TPU v7x, 128 devices: a whole 4x4x4 slice. The times are simulated.
128 devices in a mesh: col: 16 (over y, z), row: 8 (over x, core).
Axes of the slice: x: 4, y: 4, z: 4, core: 2. Of those that a mesh axis runs over, the one named last changes fastest.
Arguments:
- tiles: bfloat16 [2, 8192, 16384], P(None, 'row', 'col')
- extents: int32 [2, 8, 16], replicated, may hold values from 32 to 128
- offsets: int32 [2, 8, 16], replicated, may hold values from 0 to 127, as said below
- bands: int32 [2, 8, 16], replicated, may hold values from 0 to 8, as said below
Outputs:
- blended: float32 [2, 8192, 16384], P(None, 'row', 'col')
- weight_total: float32 [8192, 16384], P('row', 'col')
Inputs may be any that keep to these rules, and one draw needn't show every extreme that they name: Some tile has both offsets equal to 127 and some tile has both equal to 0. `bands`: entry 0 of a tile is smaller than entry 1; some tile has the band 0 to 8.
All inputs are finite; a program needn't handle non-finite values.
Results may differ from a plain program's by a relative error of at most 0.0003.
Values may be sent and summed in bfloat16 or wider, within the bound.
A program may use at most 128 MiB of HBM per device.

v0:
```python
import jax
import jax.numpy as jnp
from jax import lax
from jax.sharding import PartitionSpec as P

STRIP = 128
SPILL = 128
BLOCK = 128


eps = 1e-06


def extended(cells, sides, width):
    for axis, dim in sides:
        count = lax.axis_size(axis)
        ends = count - 1
        head = lax.slice_in_dim(cells, 0, width, axis=dim)
        tail = lax.slice_in_dim(cells, cells.shape[dim] - width, cells.shape[dim], axis=dim)
        cells = jnp.concatenate(
            [
                lax.ppermute(tail, axis, [(i, (i + 1) % count) for i in range(ends)]),
                cells,
                lax.ppermute(head, axis, [((i + 1) % count, i) for i in range(ends)]),
            ],
            axis=dim,
        )
    return cells


def from_behind(block, axis, distance):
    devices = range(lax.axis_size(axis))
    route = [(i - distance, i) for i in devices if i - distance in devices]
    return lax.ppermute(block, axis, route)


def pair_terms(former, latter, window):
    full_window = jnp.broadcast_to(window, former.shape)
    number = jnp.sum(full_window, axis=(-2, -1), keepdims=True)
    mean_former = jnp.sum(former * full_window, axis=(-2, -1), keepdims=True) / number
    mean_latter = jnp.sum(latter * full_window, axis=(-2, -1), keepdims=True) / number
    dev_former = (former - mean_former) * full_window
    dev_latter = (latter - mean_latter) * full_window
    flat_number = number[..., 0, 0]
    var_former = jnp.sum(dev_former * dev_former, axis=(-2, -1)) / flat_number
    var_latter = jnp.sum(dev_latter * dev_latter, axis=(-2, -1)) / flat_number
    covariance = jnp.sum(dev_former * dev_latter, axis=(-2, -1)) / flat_number
    weight = covariance * covariance / ((var_former + eps) * (var_latter + eps))
    log_ratio = 0.25 * (jnp.log(var_latter + eps) - jnp.log(var_former + eps))
    shift_term = 0.5 * (mean_latter - mean_former)[..., 0, 0]
    return (weight, weight * log_ratio, weight * shift_term)


def combine(right_pair, down_pair, left_pair, upper_pair):
    denominator = 1.0 + right_pair[0] + down_pair[0] + left_pair[0] + upper_pair[0]
    log_gain = (right_pair[1] + down_pair[1] - left_pair[1] - upper_pair[1]) / denominator
    offset = (right_pair[2] + down_pair[2] - left_pair[2] - upper_pair[2]) / denominator
    return (log_gain, offset)


def apply_terms(strips, log_gain, offset):
    return jnp.exp(log_gain)[:, None, None] * strips + offset[:, None, None]


def blend_weight(row_ids, col_ids, band_low, band_high, tile_px):
    half = tile_px / 2.0
    row_fade = (jnp.minimum(row_ids, tile_px - 1 - row_ids) + 1).astype(jnp.float32) / half
    col_fade = (jnp.minimum(col_ids, tile_px - 1 - col_ids) + 1).astype(jnp.float32) / half
    live = ((row_ids >= band_low * BLOCK) & (row_ids < band_high * BLOCK)).astype(jnp.float32)
    return (live * row_fade)[:, None] * col_fade[None, :]


def place_piece(
    raw_data,
    log_gain,
    offset,
    top_shift,
    left_shift,
    band_low,
    band_high,
    out_rows,
    out_cols,
    tile_px,
):
    reach = STRIP + SPILL
    planes = raw_data.shape[0]
    padded = jnp.pad(raw_data, ((0, 0), (reach, reach), (reach, reach)))
    zero = jnp.zeros((), jnp.int32)
    top_shift = jnp.asarray(top_shift, jnp.int32)
    left_shift = jnp.asarray(left_shift, jnp.int32)
    window = lax.dynamic_slice(
        padded, (zero, reach - top_shift, reach - left_shift), (planes, out_rows, out_cols)
    )
    src_rows = jnp.arange(out_rows, dtype=jnp.int32) - top_shift
    src_cols = jnp.arange(out_cols, dtype=jnp.int32) - left_shift
    row_valid = ((src_rows >= 0) & (src_rows < raw_data.shape[1])).astype(jnp.float32)
    col_valid = ((src_cols >= 0) & (src_cols < raw_data.shape[2])).astype(jnp.float32)
    weight = blend_weight(src_rows, src_cols, band_low, band_high, tile_px)
    weight = weight * row_valid[:, None] * col_valid[None, :]
    values = apply_terms(window.astype(jnp.float32), log_gain, offset) * weight[None]
    return jnp.concatenate([values, weight[None]], axis=0)


def four_pairs(own_strips, far_strips, windows):
    right_pair = pair_terms(own_strips[0], far_strips[0], windows[0])
    down_pair = pair_terms(own_strips[1], far_strips[1], windows[1])
    left_pair = pair_terms(far_strips[2], own_strips[2], windows[2])
    upper_pair = pair_terms(far_strips[3], own_strips[3], windows[3])
    return combine(right_pair, down_pair, left_pair, upper_pair)


def local(tiles, extents, offsets, bands):
    planes, tile_px, _ = tiles.shape
    row_index = lax.axis_index("row")
    col_index = lax.axis_index("col")
    padded = extended(tiles, (("col", 2), ("row", 1)), STRIP)
    width = STRIP
    own_right = tiles[:, :, tile_px - width :].astype(jnp.float32)
    own_down = tiles[:, tile_px - width :, :].astype(jnp.float32)
    own_left = tiles[:, :, :width].astype(jnp.float32)
    own_up = tiles[:, :width, :].astype(jnp.float32)
    far_right = padded[:, width : width + tile_px, width + tile_px :].astype(jnp.float32)
    far_down = padded[:, width + tile_px :, width : width + tile_px].astype(jnp.float32)
    far_left = padded[:, width : width + tile_px, :width].astype(jnp.float32)
    far_up = padded[:, :width, width : width + tile_px].astype(jnp.float32)
    left_col = jnp.maximum(col_index - 1, 0)
    upper_row = jnp.maximum(row_index - 1, 0)
    strip_ids = jnp.arange(width, dtype=jnp.int32)
    windows = (
        (strip_ids < extents[0, row_index, col_index]).astype(jnp.float32)[None, None, :],
        (strip_ids < extents[1, row_index, col_index]).astype(jnp.float32)[None, :, None],
        (strip_ids < extents[0, row_index, left_col]).astype(jnp.float32)[None, None, :],
        (strip_ids < extents[1, upper_row, col_index]).astype(jnp.float32)[None, :, None],
    )
    own_strips = (own_right, own_down, own_left, own_up)
    far_strips = (far_right, far_down, far_left, far_up)
    gain_one, level_one = four_pairs(own_strips, far_strips, windows)
    gain_terms = jnp.concatenate([gain_one, level_one])[:, None, None]
    near_terms = extended(gain_terms, (("col", 2), ("row", 1)), 1)
    places = ((1, 2), (2, 1), (1, 0), (0, 1))
    own_fixed = tuple((apply_terms(item, gain_one, level_one) for item in own_strips))
    far_fixed = tuple(
        (
            apply_terms(
                item, near_terms[:planes, spot[0], spot[1]], near_terms[planes:, spot[0], spot[1]]
            )
            for item, spot in zip(far_strips, places)
        )
    )
    gain_two, level_two = four_pairs(own_fixed, far_fixed, windows)
    log_gain = gain_one + gain_two
    level = jnp.exp(gain_two) * level_one + level_two
    own_low = bands[0, row_index, col_index]
    own_high = bands[1, row_index, col_index]
    canvas = place_piece(
        tiles,
        log_gain,
        level,
        offsets[0, row_index, col_index],
        offsets[1, row_index, col_index],
        own_low,
        own_high,
        tile_px + SPILL,
        tile_px + SPILL,
        tile_px,
    )
    section = canvas[:, :tile_px, :tile_px]
    band_in = from_behind(canvas[:, :, tile_px:], "col", 1)
    section = section.at[:, :, :SPILL].add(band_in[:, :tile_px])
    lower_part = canvas[:, tile_px:, :tile_px].at[:, :, :SPILL].add(band_in[:, tile_px:])
    lower_in = from_behind(lower_part, "row", 1)
    section = section.at[:, :SPILL, :].add(lower_in)
    return (section[:planes], section[planes])


def solution(mesh):
    return jax.shard_map(
        local,
        mesh=mesh,
        in_specs=(P(None, "row", "col"), P(), P(), P()),
        out_specs=(P(None, "row", "col"), P("row", "col")),
        check_vma=False,
    )
```

profile of v0, /device:TPU:28, one launch (start us, length us, event | category | flops | bytes accessed | tf_op | source)
XLA Modules:
  0.0 156.8 jit_solution(13975208082393259920)
XLA Ops:
  0.6 1.3 fusion.132
  1.9 3.8 %collective-permute-start.1 = (bf16[2,1024,128]{2,1,0:T(8,128)(2,1)S(1)}, bf16[2,1024,128]{2,1,0:T(8,128)(2,1)S(1)}, u32[]{:S(2)}, u32[]{:S(2)}) collective-permute-start(bf16[2,1024,128]{2,1,0:T(8,128)(2,1)S(1)} %get-tuple-element.99), channel_id=1, source_target_pairs={{0,8},{8,16},{16,24},{24,32},{32,40},{40,48},{48,56},{56,64},{64,7... | collective-permute-start | bytes 1572872 | tf_op jit(solution)/shard_map/ppermute | solution.py:22
  5.8 4.2 %collective-permute-start = (bf16[2,1024,128]{2,1,0:T(8,128)(2,1)S(1)}, bf16[2,1024,128]{2,1,0:T(8,128)(2,1)S(1)}, u32[]{:S(2)}, u32[]{:S(2)}) collective-permute-start(bf16[2,1024,128]{2,1,0:T(8,128)(2,1)S(1)} %get-tuple-element.98), channel_id=1, source_target_pairs={{8,0},{16,8},{24,16},{32,24},{40,32},{48,40},{56,48},{64,56},{72,6... | collective-permute-start | bytes 1572872 | tf_op jit(solution)/shard_map/ppermute | solution.py:24
  10.0 1.4 constant_dynamic-slice_fusion.5
  11.4 0.7 fusion.118
  12.0 1.3 fusion.127
  13.4 1.4 constant_dynamic-slice_fusion
  16.1 0.7 fusion.115
  16.8 3.1 %multiply_multiply_fusion.1 = f32[1152,1152]{1,0:T(8,128)} fusion(f32[1152]{0:T(1024)S(1)} %get-tuple-element.137, f32[1152]{0:T(1024)S(1)} %get-tuple-element.136, f32[1152]{0:T(1024)S(1)} %fusion.118, f32[1152]{0:T(1024)S(1)} %fusion.115), kind=kLoop, calls=%fused_computation.12 | loop fusion | flops 3981312 | bytes 5326848 | tf_op jit(solution)/shard_map/mul | solution.py:99
  20.0 3.1 %multiply_multiply_fusion = f32[1,1152,1152]{2,1,0:T(8,128)} fusion(f32[1152]{0:T(1024)S(1)} %get-tuple-element.137, f32[1152]{0:T(1024)S(1)} %get-tuple-element.136, f32[1152]{0:T(1024)S(1)} %fusion.118, f32[1152]{0:T(1024)S(1)} %fusion.115), kind=kLoop, calls=%fused_computation.11 | loop fusion | flops 3981312 | bytes 5326848 | tf_op jit(solution)/shard_map/mul | solution.py:99
  25.8 0.6 compare_convert_fusion.2
  26.4 0.6 compare_convert_fusion
  27.0 0.6 compare_convert_fusion.3
  27.6 0.6 compare_convert_fusion.1
  28.2 0.0 collective-permute-done.1
  28.3 0.1 constant_dynamic-update-slice_fusion.2
  28.4 0.0 copy-start.1
  28.4 2.8 %constant_dynamic-update-slice_fusion.1 = bf16[2,1024,1280]{2,1,0:T(8,128)(2,1)S(1)} fusion(bf16[2,1024,1280]{2,1,0:T(8,128)(2,1)S(1)} %constant_dynamic-update-slice_fusion.2, bf16[2,1024,1024]{2,1,0:T(8,128)(2,1)} %param.10), kind=kLoop, calls=%fused_computation.166 | loop fusion | bytes 8388608
  31.2 0.0 collective-permute-done
  31.2 0.1 constant_dynamic-update-slice_fusion
  31.3 0.1 fusion.131
  31.4 1.9 %collective-permute-start.3 = (bf16[2,128,1280]{2,1,0:T(8,128)(2,1)S(1)}, bf16[2,128,1280]{2,1,0:T(8,128)(2,1)S(1)}, u32[]{:S(2)}, u32[]{:S(2)}) collective-permute-start(bf16[2,128,1280]{2,1,0:T(8,128)(2,1)S(1)} %get-tuple-element.97), channel_id=1, source_target_pairs={{0,1},{1,2},{2,3},{3,4},{4,5},{5,6},{6,7},{8,9},{9,10},{10,11},{11... | collective-permute-start | bytes 1966088 | tf_op jit(solution)/shard_map/ppermute | solution.py:22
  33.3 3.6 %collective-permute-start.2 = (bf16[2,128,1280]{2,1,0:T(8,128)(2,1)S(1)}, bf16[2,128,1280]{2,1,0:T(8,128)(2,1)S(1)}, u32[]{:S(2)}, u32[]{:S(2)}) collective-permute-start(bf16[2,128,1280]{2,1,0:T(8,128)(2,1)S(1)} %get-tuple-element.96), channel_id=1, source_target_pairs={{1,0},{2,1},{3,2},{4,3},{5,4},{6,5},{7,6},{9,8},{10,9},{11,10},{12... | collective-permute-start | bytes 1966088 | tf_op jit(solution)/shard_map/ppermute | solution.py:24
  37.0 0.4 fusion.7
  37.4 0.9 fusion.12
  38.3 0.8 fusion.77
  39.1 4.2 %collective-permute-done.3 = bf16[2,128,1280]{2,1,0:T(8,128)(2,1)S(1)} collective-permute-done((bf16[2,128,1280]{2,1,0:T(8,128)(2,1)S(1)}, bf16[2,128,1280]{2,1,0:T(8,128)(2,1)S(1)}, u32[]{:S(2)}, u32[]{:S(2)}) %collective-permute-start.3) | collective-permute-done | bytes 655392 | tf_op jit(solution)/shard_map/ppermute | solution.py:22
  43.3 1.8 %collective-permute-done.2 = bf16[2,128,1280]{2,1,0:T(8,128)(2,1)S(1)} collective-permute-done((bf16[2,128,1280]{2,1,0:T(8,128)(2,1)S(1)}, bf16[2,128,1280]{2,1,0:T(8,128)(2,1)S(1)}, u32[]{:S(2)}, u32[]{:S(2)}) %collective-permute-start.2) | collective-permute-done | bytes 655392 | tf_op jit(solution)/shard_map/ppermute | solution.py:24
  45.1 0.8 fusion.33
  45.9 1.3 fusion.38
  47.3 0.1 maximum_bitcast_fusion
  47.4 3.9 %collective-permute-start.4 = (f32[4,1,1]{0,2,1:T(1,128)S(1)}, f32[4,1,1]{0,2,1:T(1,128)S(1)}, u32[]{:S(2)}, u32[]{:S(2)}) collective-permute-start(f32[4,1,1]{0,2,1:T(1,128)S(1)} %maximum_bitcast_fusion), channel_id=1, source_target_pairs={{8,0},{16,8},{24,16},{32,24},{40,32},{48,40},{56,48},{64,56},{72,6... | collective-permute-start | bytes 56 | tf_op jit(solution)/shard_map/ppermute | solution.py:24
  51.3 1.9 %collective-permute-start.5 = (f32[4,1,1]{0,2,1:T(1,128)S(1)}, f32[4,1,1]{0,2,1:T(1,128)S(1)}, u32[]{:S(2)}, u32[]{:S(2)}) collective-permute-start(f32[4,1,1]{0,2,1:T(1,128)S(1)} %maximum_bitcast_fusion), channel_id=1, source_target_pairs={{0,8},{8,16},{16,24},{24,32},{32,40},{40,48},{48,56},{56,64},{64,7... | collective-permute-start | bytes 56 | tf_op jit(solution)/shard_map/ppermute | solution.py:22
  53.2 0.0 collective-permute-done.4
  53.2 5.6 %collective-permute-done.5 = f32[4,1,1]{0,2,1:T(1,128)S(1)} collective-permute-done((f32[4,1,1]{0,2,1:T(1,128)S(1)}, f32[4,1,1]{0,2,1:T(1,128)S(1)}, u32[]{:S(2)}, u32[]{:S(2)}) %collective-permute-start.5) | collective-permute-done | bytes 48 | tf_op jit(solution)/shard_map/ppermute | solution.py:22
  58.8 2.4 %collective-permute-start.6 = (f32[4,1,3]{0,2,1:T(4,128)S(1)}, f32[4,1,3]{0,2,1:T(4,128)S(1)}, u32[]{:S(2)}, u32[]{:S(2)}) collective-permute-start(f32[4,1,3]{0,2,1:T(4,128)S(1)} %pad_maximum_fusion.1), channel_id=1, source_target_pairs={{1,0},{2,1},{3,2},{4,3},{5,4},{6,5},{7,6},{9,8},{10,9},{11,10},{12... | collective-permute-start | bytes 152 | tf_op jit(solution)/shard_map/ppermute | solution.py:24
  61.2 2.1 %collective-permute-start.7 = (f32[4,1,3]{0,2,1:T(4,128)S(1)}, f32[4,1,3]{0,2,1:T(4,128)S(1)}, u32[]{:S(2)}, u32[]{:S(2)}) collective-permute-start(f32[4,1,3]{0,2,1:T(4,128)S(1)} %pad_maximum_fusion.1), channel_id=1, source_target_pairs={{0,1},{1,2},{2,3},{3,4},{4,5},{5,6},{6,7},{8,9},{9,10},{10,11},{11... | collective-permute-start | bytes 152 | tf_op jit(solution)/shard_map/ppermute | solution.py:22
  63.4 0.1 exponential_bitcast_fusion.3
  63.4 0.6 fusion.16
  64.0 0.1 exponential_bitcast_fusion.1
  64.1 1.2 fusion.21
  65.2 0.8 fusion.84
  66.1 0.0 collective-permute-done.6
  66.1 0.1 exponential_bitcast_fusion.2
  66.2 0.6 fusion.42
  66.7 0.0 collective-permute-done.7
  66.7 0.1 exponential_bitcast_fusion
  66.8 1.2 fusion.47
  68.0 0.8 fusion.110
  68.9 0.0 slice-start.1
  68.9 12.2 %add_multiply_fusion = f32[2,1152,1152]{2,1,0:T(8,128)} fusion(s32[]{:T(128)S(6)} %select_n.10, s32[]{:T(128)S(6)} %select_n.11, bf16[2,1024,1024]{2,1,0:T(8,128)(2,1)} %param.10, f32[1152,1152]{1,0:T(8,128)} %multiply_multiply_fusion.1, f32[2]{0:T(128)S(1)} %divide_add_fusion, f32[2]{0:T(128)S(1)} %get-tuple-element.84), kind=kLoop, calls=%fused_computation.9 | loop fusion | flops 10616832 | bytes 20119576 | tf_op jit(solution)/shard_map/mul | solution.py:100
  81.1 0.0 slice-done
  81.1 1.5 fusion.1
  82.7 2.3 %collective-permute-start.8 = (f32[3,1152,128]{2,1,0:T(8,128)S(1)}, f32[3,1152,128]{2,1,0:T(8,128)S(1)}, u32[]{:S(2)}, u32[]{:S(2)}) collective-permute-start(f32[3,1152,128]{2,1,0:T(8,128)S(1)} %fusion.1), channel_id=1, source_target_pairs={{0,8},{8,16},{16,24},{24,32},{32,40},{40,48},{48,56},{56,64},{64,7... | collective-permute-start | bytes 5308424 | tf_op jit(solution)/shard_map/ppermute | solution.py:34
  85.0 0.5 copy-done
  85.5 0.2 fusion.2
  85.7 42.4 %collective-permute-done.8 = f32[3,1152,128]{2,1,0:T(8,128)S(1)} collective-permute-done((f32[3,1152,128]{2,1,0:T(8,128)S(1)}, f32[3,1152,128]{2,1,0:T(8,128)S(1)}, u32[]{:S(2)}, u32[]{:S(2)}) %collective-permute-start.8) | collective-permute-done | bytes 1769504 | tf_op jit(solution)/shard_map/ppermute | solution.py:34
  128.1 2.0 %collective-permute-start.9 = (f32[3,128,1024]{2,1,0:T(8,128)S(1)}, f32[3,128,1024]{2,1,0:T(8,128)S(1)}, u32[]{:S(2)}, u32[]{:S(2)}) collective-permute-start(f32[3,128,1024]{2,1,0:T(8,128)S(1)} %fusion.111), channel_id=1, source_target_pairs={{0,1},{1,2},{2,3},{3,4},{4,5},{5,6},{6,7},{8,9},{9,10},{10,11},{11... | collective-permute-start | bytes 4718600 | tf_op jit(solution)/shard_map/ppermute | solution.py:34
  130.2 1.8 %fusion = f32[3,1024,1024]{2,1,0:T(8,128)S(1)} fusion(f32[2,1152,1152]{2,1,0:T(8,128)S(1)} %copy-done, f32[1,1152,1152]{2,1,0:T(8,128)S(1)} %bitcast.29), kind=kLoop, calls=%fused_computation.8 | loop fusion | flops 3145728 | bytes 28508160 | tf_op jit(solution)/shard_map/concatenate | solution.py:101
  132.0 0.2 fusion.5
  132.2 17.6 %collective-permute-done.9 = f32[3,128,1024]{2,1,0:T(8,128)S(1)} collective-permute-done((f32[3,128,1024]{2,1,0:T(8,128)S(1)}, f32[3,128,1024]{2,1,0:T(8,128)S(1)}, u32[]{:S(2)}, u32[]{:S(2)}) %collective-permute-start.9) | collective-permute-done | bytes 1572896 | tf_op jit(solution)/shard_map/ppermute | solution.py:34
  149.9 0.4 fusion.6
  150.3 4.2 %slice.186 = f32[2,1024,1024]{2,1,0:T(8,128)} slice(f32[3,1024,1024]{2,1,0:T(8,128)S(1)} %fusion.6), slice={[0:2], [0:1024], [0:1024]} | slice | bytes 16777216 | tf_op jit(solution)/shard_map/slice | solution.py:173
  154.5 2.3 %slice_bitcast_fusion = f32[1024,1024]{1,0:T(8,128)} fusion(f32[3,1024,1024]{2,1,0:T(8,128)S(1)} %fusion.6), kind=kLoop, calls=%fused_computation.13 | loop fusion | bytes 8388608 | tf_op jit(solution)/shard_map/squeeze | solution.py:173
  (19 shorter events, 0.2 us)
Async XLA Ops:
  1.9 26.3 %collective-permute-start.1 = (bf16[2,1024,128]{2,1,0:T(8,128)(2,1)S(1)}, bf16[2,1024,128]{2,1,0:T(8,128)(2,1)S(1)}, u32[]{:S(2)}, u32[]{:S(2)}) collective-permute-start(bf16[2,1024,128]{2,1,0:T(8,128)(2,1)S(1)} %get-tuple-element.99), channel_id=1, source_target_pairs={{0,8},{8,16},{16,24},{24,32},{32,40},{40,48},{48,56},{56,64},{64,7... | collective-permute-start | bytes 1572872 | tf_op jit(solution)/shard_map/ppermute | solution.py:22
  5.8 25.4 %collective-permute-start = (bf16[2,1024,128]{2,1,0:T(8,128)(2,1)S(1)}, bf16[2,1024,128]{2,1,0:T(8,128)(2,1)S(1)}, u32[]{:S(2)}, u32[]{:S(2)}) collective-permute-start(bf16[2,1024,128]{2,1,0:T(8,128)(2,1)S(1)} %get-tuple-element.98), channel_id=1, source_target_pairs={{8,0},{16,8},{24,16},{32,24},{40,32},{48,40},{56,48},{64,56},{72,6... | collective-permute-start | bytes 1572872 | tf_op jit(solution)/shard_map/ppermute | solution.py:24
  28.4 8.6 %copy-start.1 = (bf16[2,1024,1024]{2,1,0:T(8,128)(2,1)S(1)}, bf16[2,1024,1024]{2,1,0:T(8,128)(2,1)}, u32[]{:S(2)}) copy-start(bf16[2,1024,1024]{2,1,0:T(8,128)(2,1)} %param.10) | copy-start | bytes 12582916
  31.4 11.9 %collective-permute-start.3 = (bf16[2,128,1280]{2,1,0:T(8,128)(2,1)S(1)}, bf16[2,128,1280]{2,1,0:T(8,128)(2,1)S(1)}, u32[]{:S(2)}, u32[]{:S(2)}) collective-permute-start(bf16[2,128,1280]{2,1,0:T(8,128)(2,1)S(1)} %get-tuple-element.97), channel_id=1, source_target_pairs={{0,1},{1,2},{2,3},{3,4},{4,5},{5,6},{6,7},{8,9},{9,10},{10,11},{11... | collective-permute-start | bytes 1966088 | tf_op jit(solution)/shard_map/ppermute | solution.py:22
  33.3 11.7 %collective-permute-start.2 = (bf16[2,128,1280]{2,1,0:T(8,128)(2,1)S(1)}, bf16[2,128,1280]{2,1,0:T(8,128)(2,1)S(1)}, u32[]{:S(2)}, u32[]{:S(2)}) collective-permute-start(bf16[2,128,1280]{2,1,0:T(8,128)(2,1)S(1)} %get-tuple-element.96), channel_id=1, source_target_pairs={{1,0},{2,1},{3,2},{4,3},{5,4},{6,5},{7,6},{9,8},{10,9},{11,10},{12... | collective-permute-start | bytes 1966088 | tf_op jit(solution)/shard_map/ppermute | solution.py:24
  47.4 5.8 %collective-permute-start.4 = (f32[4,1,1]{0,2,1:T(1,128)S(1)}, f32[4,1,1]{0,2,1:T(1,128)S(1)}, u32[]{:S(2)}, u32[]{:S(2)}) collective-permute-start(f32[4,1,1]{0,2,1:T(1,128)S(1)} %maximum_bitcast_fusion), channel_id=1, source_target_pairs={{8,0},{16,8},{24,16},{32,24},{40,32},{48,40},{56,48},{64,56},{72,6... | collective-permute-start | bytes 56 | tf_op jit(solution)/shard_map/ppermute | solution.py:24
  51.3 7.5 %collective-permute-start.5 = (f32[4,1,1]{0,2,1:T(1,128)S(1)}, f32[4,1,1]{0,2,1:T(1,128)S(1)}, u32[]{:S(2)}, u32[]{:S(2)}) collective-permute-start(f32[4,1,1]{0,2,1:T(1,128)S(1)} %maximum_bitcast_fusion), channel_id=1, source_target_pairs={{0,8},{8,16},{16,24},{24,32},{32,40},{40,48},{48,56},{56,64},{64,7... | collective-permute-start | bytes 56 | tf_op jit(solution)/shard_map/ppermute | solution.py:22
  58.8 7.3 %collective-permute-start.6 = (f32[4,1,3]{0,2,1:T(4,128)S(1)}, f32[4,1,3]{0,2,1:T(4,128)S(1)}, u32[]{:S(2)}, u32[]{:S(2)}) collective-permute-start(f32[4,1,3]{0,2,1:T(4,128)S(1)} %pad_maximum_fusion.1), channel_id=1, source_target_pairs={{1,0},{2,1},{3,2},{4,3},{5,4},{6,5},{7,6},{9,8},{10,9},{11,10},{12... | collective-permute-start | bytes 152 | tf_op jit(solution)/shard_map/ppermute | solution.py:24
  61.2 5.5 %collective-permute-start.7 = (f32[4,1,3]{0,2,1:T(4,128)S(1)}, f32[4,1,3]{0,2,1:T(4,128)S(1)}, u32[]{:S(2)}, u32[]{:S(2)}) collective-permute-start(f32[4,1,3]{0,2,1:T(4,128)S(1)} %pad_maximum_fusion.1), channel_id=1, source_target_pairs={{0,1},{1,2},{2,3},{3,4},{4,5},{5,6},{6,7},{8,9},{9,10},{10,11},{11... | collective-permute-start | bytes 152 | tf_op jit(solution)/shard_map/ppermute | solution.py:22
  68.0 13.1 %slice-start = ((s8[5308416]{0:T(1024)(128)(4,1)}), s8[4194304]{0:T(1024)(128)(4,1)S(1)}, s32[]{:S(2)}) async-start(s8[5308416]{0:T(1024)(128)(4,1)} %bitcast.28), calls=%async_computation | async-start | bytes 8388608
  68.9 12.2 %slice-start.1 = ((s8[5308416]{0:T(1024)(128)(4,1)}), s8[1114112]{0:T(1024)(128)(4,1)S(1)}, s32[]{:S(2)}) async-start(s8[5308416]{0:T(1024)(128)(4,1)} %bitcast.28), calls=%async_computation.1 | async-start | bytes 2228224
  81.1 4.4 %copy-start = (f32[2,1152,1152]{2,1,0:T(8,128)S(1)}, f32[2,1152,1152]{2,1,0:T(8,128)}, u32[]{:S(2)}) copy-start(f32[2,1152,1152]{2,1,0:T(8,128)} %add_multiply_fusion) | copy-start | bytes 31850500
  82.7 45.4 %collective-permute-start.8 = (f32[3,1152,128]{2,1,0:T(8,128)S(1)}, f32[3,1152,128]{2,1,0:T(8,128)S(1)}, u32[]{:S(2)}, u32[]{:S(2)}) collective-permute-start(f32[3,1152,128]{2,1,0:T(8,128)S(1)} %fusion.1), channel_id=1, source_target_pairs={{0,8},{8,16},{16,24},{24,32},{32,40},{40,48},{48,56},{56,64},{64,7... | collective-permute-start | bytes 5308424 | tf_op jit(solution)/shard_map/ppermute | solution.py:34
  128.1 21.7 %collective-permute-start.9 = (f32[3,128,1024]{2,1,0:T(8,128)S(1)}, f32[3,128,1024]{2,1,0:T(8,128)S(1)}, u32[]{:S(2)}, u32[]{:S(2)}) collective-permute-start(f32[3,128,1024]{2,1,0:T(8,128)S(1)} %fusion.111), channel_id=1, source_target_pairs={{0,1},{1,2},{2,3},{3,4},{4,5},{5,6},{6,7},{8,9},{9,10},{10,11},{11... | collective-permute-start | bytes 4718600 | tf_op jit(solution)/shard_map/ppermute | solution.py:34
where the time goes:
time: 157 us
  waiting for transfers between devices  71.6 us (46%)
  other arithmetic  37.4 us (24%)
  starting transfers between devices  28.3 us (18%)
  local copies, waits for them, and re-layouts  14.6 us (9%)
  between operations  4.91 us (3%)
    ppermute x2, waiting for transfers between devices, from_behind(): return lax.ppermute(block, axis, route)  60 us
    ppermute x4, starting transfers between devices, extended(): lax.ppermute(head, axis, [((i + 1) % count, i) for i in range(ends)])  14.2 us
    mul x1, other arithmetic, place_piece(): apply_terms(window.astype(jnp.float32), log_gain, offset) * weight[None]  12.2 us
    ppermute x4, waiting for transfers between devices, extended(): lax.ppermute(tail, axis, [(i, (i + 1) % count) for i in range(ends)])  9.83 us
    ppermute x4, starting transfers between devices, extended(): lax.ppermute(tail, axis, [(i, (i + 1) % count) for i in range(ends)])  9.79 us
    mul x2, other arithmetic, place_piece(): weight = weight * row_valid[:, None] * col_valid[None, :]  6.27 us
    reduce_sum x4, other arithmetic, pair_terms(): var_former = jnp.sum(dev_former * dev_former, axis=(-2, -1)) / flat_number  4.59 us
    ppermute x2, starting transfers between devices, from_behind(): return lax.ppermute(block, axis, route)  4.36 us
  transfers between devices with their start and end apart: 10, of which 5 were waited for; matrix products, arithmetic and copies ran while one was open for 16% of the time, Pallas kernels for 0%

commit v1 on v0

v1 whole, which is shorter than its diff:
```python
import jax
import jax.numpy as jnp
from jax import lax
from jax.experimental import pallas as pl
from jax.experimental.pallas import tpu as pltpu
from jax.sharding import PartitionSpec as P

STRIP = 128
SPILL = 128
BLOCK = 128
LANES = 128
PLANES = 2
EPS = 1e-6
MESH = pl.DeviceIdType.MESH
F32 = jnp.float32

RIGHT_1, LEFT_1, DOWN_1, UP_1, RIGHT_2, DOWN_2, CORNER = range(7)
STATS, COV, FIRST, FINAL = 7, 11, 15, 19
COPIES = 22


def rows_of(per_plane):
    return jnp.concatenate(
        [jnp.broadcast_to(jnp.sum(a, keepdims=True), (1, LANES)) for a in per_plane], axis=0
    )


def fold(x):
    return jnp.sum(x.reshape(x.shape[0] // 8, 8, x.shape[1]), axis=0)


def sum_tall(ref, plane, mask, term):
    size = 128

    def body(i, acc):
        x = ref[plane, pl.ds(pl.multiple_of(i * size, size), size), :].astype(F32)
        return acc + fold(term(x))

    acc = lax.fori_loop(0, ref.shape[1] // size, body, jnp.zeros((8, LANES), F32))
    return jnp.where(mask, acc, 0.0)


def sum_wide(ref, plane, extent, term):
    size = 16
    ids = lax.broadcasted_iota(jnp.int32, (size, LANES), 0)

    def body(i, acc):
        x = ref[plane, pl.ds(pl.multiple_of(i * size, size), size), :].astype(F32)
        t = term(x)
        part = sum(t[:, k : k + LANES] for k in range(0, x.shape[1], LANES))
        return acc + fold(jnp.where(ids + i * size < extent, part, 0.0))

    return lax.fori_loop(0, STRIP // size, body, jnp.zeros((8, LANES), F32))


def cov_tall(own, own_start, other, own_mean, other_mean, plane, mask):
    size = 128

    def body(i, acc):
        start = pl.multiple_of(i * size, size)
        x = own[plane, pl.ds(own_start + start, size), :].astype(F32) - own_mean
        y = other[plane, pl.ds(start, size), :].astype(F32) - other_mean
        return acc + fold(x * y)

    acc = lax.fori_loop(0, other.shape[1] // size, body, jnp.zeros((8, LANES), F32))
    return jnp.where(mask, acc, 0.0)


def cov_wide(own, own_start, other, own_mean, other_mean, plane, extent):
    size = 16
    width = other.shape[2]
    ids = lax.broadcasted_iota(jnp.int32, (size, LANES), 0)

    def body(i, acc):
        start = pl.multiple_of(i * size, size)
        x = own[plane, pl.ds(start, size), own_start : own_start + width].astype(F32)
        y = other[plane, pl.ds(start, size), :].astype(F32)
        part = sum(
            (x[:, k : k + LANES] - own_mean) * (y[:, k : k + LANES] - other_mean)
            for k in range(0, width, LANES)
        )
        return acc + fold(jnp.where(ids + i * size < extent, part, 0.0))

    return lax.fori_loop(0, STRIP // size, body, jnp.zeros((8, LANES), F32))


def pair_terms(mean_a, var_a, mean_b, var_b, cov, valid):
    weight = cov * cov / ((var_a + EPS) * (var_b + EPS))
    ratio = 0.25 * (jnp.log(var_b + EPS) - jnp.log(var_a + EPS))
    shift = 0.5 * (mean_b - mean_a)
    return tuple(jnp.where(valid, t, 0.0) for t in (weight, weight * ratio, weight * shift))


def combine(right, left, down, upper):
    total = 1.0 + right[0] + down[0] + left[0] + upper[0]
    log_gain = (right[1] + down[1] - left[1] - upper[1]) / total
    level = (right[2] + down[2] - left[2] - upper[2]) / total
    return log_gain, level


def exchange_kernel(
    extents, tiles, left_in, up_in, corner_in, terms,
    strip_r, strip_l, strip_d, strip_u, half_l, half_r, half_u, half_d,
    stats_out, stats_in, cov_out, cov_in, first_out, first_in, final_out, final_in,
    load_sem, send_sem, recv_sem,
):
    n_col, n_row = lax.axis_size("col"), lax.axis_size("row")
    col, row = lax.axis_index("col"), lax.axis_index("row")
    right, left = lax.rem(col + 1, n_col), lax.rem(col + n_col - 1, n_col)
    down, up = lax.rem(row + 1, n_row), lax.rem(row + n_row - 1, n_row)
    tile = tiles.shape[1]
    half = tile // 2
    edge = tile - STRIP
    four = ({"col": right}, {"col": left}, {"row": down}, {"row": up})
    diag = {"col": right, "row": down}
    back = {"col": left, "row": up}

    barrier = pltpu.get_barrier_semaphore()
    for place in (*four, diag, back):
        pl.semaphore_signal(barrier, inc=1, device_id=place, device_id_type=MESH)

    own = (strip_r, strip_l, strip_d, strip_u)
    views = (
        tiles.at[:, :, edge:],
        tiles.at[:, :, :STRIP],
        tiles.at[:, edge:, :],
        tiles.at[:, :STRIP, :],
    )
    loads = [pltpu.make_async_copy(v, s, load_sem.at[k]) for k, (v, s) in enumerate(zip(views, own))]
    for load in loads:
        load.start()

    pl.semaphore_wait(barrier, 6)

    def send(index, src, dst, place):
        copy = pltpu.make_async_remote_copy(
            src_ref=src,
            dst_ref=dst,
            send_sem=send_sem.at[index],
            recv_sem=recv_sem.at[index],
            device_id=place,
            device_id_type=MESH,
        )
        copy.start()
        return copy

    bulk = [
        send(RIGHT_1, tiles.at[:, half:, edge:], half_l, four[0]),
        send(LEFT_1, tiles.at[:, :half, :STRIP], half_r, four[1]),
        send(DOWN_1, tiles.at[:, edge:, half:], half_u, four[2]),
        send(UP_1, tiles.at[:, :STRIP, :half], half_d, four[3]),
    ]

    ext = (
        extents[0, row, col],
        extents[0, row, left],
        extents[1, row, col],
        extents[1, up, col],
    )
    valid = (col < n_col - 1, col > 0, row < n_row - 1, row > 0)
    lanes = lax.broadcasted_iota(jnp.int32, (8, LANES), 1)
    masks = (lanes < ext[0], lanes < ext[1])
    numbers = [(e * tile).astype(F32) for e in ext]

    means, variances = [], []
    for side in range(4):
        loads[side].wait()
        ref = own[side]
        reduce = sum_tall if side < 2 else sum_wide
        window = masks[side] if side < 2 else ext[side]
        mean = rows_of([reduce(ref, p, window, lambda x: x) for p in range(PLANES)]) / numbers[side]

        def square(p):
            m = mean[p : p + 1, :]

            def term(x):
                d = x - (m if side < 2 else m[:, :1])
                return d * d

            return reduce(ref, p, window, term)

        var = rows_of([square(p) for p in range(PLANES)]) / numbers[side]
        means.append(mean)
        variances.append(var)
        stats_out[side, 0:2, :] = mean
        stats_out[side, 2:4, :] = var

    opposite = (1, 0, 3, 2)
    small = [send(STATS + s, stats_out.at[s], stats_in.at[opposite[s]], four[s]) for s in range(4)]
    for copy in small:
        copy.wait()
    far_means = [stats_in[s, 0:2, :] for s in range(4)]
    far_vars = [stats_in[s, 2:4, :] for s in range(4)]

    received = (half_r, half_l, half_d, half_u)
    starts = (0, half, 0, half)
    bulk[1].wait()
    bulk[0].wait()
    bulk.append(send(RIGHT_2, tiles.at[:, :half, edge:], left_in.at[:, :half, :], four[0]))
    bulk.append(send(CORNER, half_l.at[:, half - STRIP :, :], corner_in, four[2]))
    bulk[3].wait()
    bulk[2].wait()
    bulk.append(send(DOWN_2, tiles.at[:, edge:, :half], up_in.at[:, :, :half], four[2]))
    keep = [
        pltpu.make_async_copy(half_l, left_in.at[:, half:, :], load_sem.at[4]),
        pltpu.make_async_copy(half_u, up_in.at[:, :, half:], load_sem.at[5]),
    ]
    for copy in keep:
        copy.start()

    for side in range(4):
        function = cov_tall if side < 2 else cov_wide
        window = masks[side] if side < 2 else ext[side]
        cov_out[side, 0:2, :] = rows_of(
            [
                function(
                    own[side],
                    starts[side],
                    received[side],
                    means[side][p : p + 1, :],
                    far_means[side][p : p + 1, :],
                    p,
                    window,
                )
                for p in range(PLANES)
            ]
        )
    small = [send(COV + s, cov_out.at[s], cov_in.at[opposite[s]], four[s]) for s in range(4)]
    for copy in small:
        copy.wait()
    cov = [(cov_out[s, 0:2, :] + cov_in[s, 0:2, :]) / numbers[s] for s in range(4)]

    def tile_terms(near_means, near_vars, distant_means, distant_vars, covs):
        parts = []
        for s in range(4):
            near, far = (near_means[s], near_vars[s]), (distant_means[s], distant_vars[s])
            first, second = (near, far) if s in (0, 2) else (far, near)
            parts.append(pair_terms(*first, *second, covs[s], valid[s]))
        return combine(*parts)

    gain_one, level_one = tile_terms(means, variances, far_means, far_vars, cov)
    first_out[0:2, :] = gain_one
    first_out[2:4, :] = level_one
    small = [send(FIRST + s, first_out, first_in.at[opposite[s]], four[s]) for s in range(4)]
    scale = jnp.exp(gain_one)
    near_means = [scale * m + level_one for m in means]
    near_vars = [scale * (scale * v) for v in variances]
    for copy in small:
        copy.wait()
    far_scale = [jnp.exp(first_in[s, 0:2, :]) for s in range(4)]
    far_level = [first_in[s, 2:4, :] for s in range(4)]
    gain_two, level_two = tile_terms(
        near_means,
        near_vars,
        [far_scale[s] * far_means[s] + far_level[s] for s in range(4)],
        [far_scale[s] * (far_scale[s] * far_vars[s]) for s in range(4)],
        [scale * (far_scale[s] * cov[s]) for s in range(4)],
    )
    gain = jnp.exp(gain_one + gain_two)
    level = jnp.exp(gain_two) * level_one + level_two
    final_out[0:2, :] = gain
    final_out[2:4, :] = level
    small = [
        send(FINAL + k, final_out, final_in.at[k], place)
        for k, place in enumerate((four[0], four[2], diag))
    ]
    terms[0, 0:2, :] = gain
    terms[0, 2:4, :] = level
    for copy in small:
        copy.wait()
    for k in range(3):
        terms[k + 1, :, :] = final_in[k]
    for copy in bulk[4:]:
        copy.wait()
    for copy in keep:
        copy.wait()


def exchange(tiles, extents):
    planes, tile, _ = tiles.shape
    dtype = tiles.dtype
    half = tile // 2
    tall = pltpu.VMEM((planes, tile, STRIP), dtype)
    wide = pltpu.VMEM((planes, STRIP, tile), dtype)
    half_tall = pltpu.VMEM((planes, half, STRIP), dtype)
    half_wide = pltpu.VMEM((planes, STRIP, half), dtype)
    message = pltpu.VMEM((4, 4, LANES), F32)
    single = pltpu.VMEM((4, LANES), F32)
    any_space = pl.BlockSpec(memory_space=pl.ANY)
    return pl.pallas_call(
        exchange_kernel,
        name="exchange",
        out_shape=(
            jax.ShapeDtypeStruct((planes, tile, STRIP), dtype),
            jax.ShapeDtypeStruct((planes, STRIP, tile), dtype),
            jax.ShapeDtypeStruct((planes, STRIP, STRIP), dtype),
            jax.ShapeDtypeStruct((4, 4, LANES), F32),
        ),
        in_specs=[pl.BlockSpec(memory_space=pltpu.SMEM), any_space],
        out_specs=(any_space, any_space, any_space, pl.BlockSpec(memory_space=pltpu.VMEM)),
        scratch_shapes=[
            tall, tall, wide, wide, half_tall, half_tall, half_wide, half_wide,
            message, message, message, message, single, message, single, message,
            pltpu.SemaphoreType.DMA((6,)),
            pltpu.SemaphoreType.DMA((COPIES,)),
            pltpu.SemaphoreType.DMA((COPIES,)),
        ],
        compiler_params=pltpu.CompilerParams(
            collective_id=0, has_side_effects=True, vmem_limit_bytes=32 * 1024 * 1024
        ),
    )(extents, tiles)


def fade(ids, limit, tile):
    steps = jnp.minimum(ids, tile - 1 - ids) + 1
    return jnp.where(limit, steps.astype(F32) * (2.0 / tile), 0.0)


def blend_kernel(
    places, offsets, bands, tiles, left_in, up_in, corner_in, terms, blended, weights,
    raw, raw_left, raw_up, raw_corner, moved, moved_left, moved_up, moved_corner, sem,
):
    step = pl.program_id(0)
    tile = raw.shape[1]
    blocks = tile // LANES
    rows = weights.shape[0]
    lanes = lax.broadcasted_iota(jnp.int32, (rows, LANES), 1)
    lines = lax.broadcasted_iota(jnp.int32, (rows, LANES), 0)
    row, col = places[0], places[1]
    up, left = jnp.maximum(row - 1, 0), jnp.maximum(col - 1, 0)

    def settings(r, c):
        return offsets[0, r, c], offsets[1, r, c], bands[0, r, c] * BLOCK, bands[1, r, c] * BLOCK

    def piece(k):
        part = pl.ds(pl.multiple_of(k * rows, rows), rows)
        return pltpu.make_async_copy(tiles.at[:, part, :], raw.at[:, part, :], sem.at[k])

    others = [
        pltpu.make_async_copy(src, dst, sem.at[blocks + k])
        for k, (src, dst) in enumerate(
            ((left_in, raw_left), (up_in, raw_up), (corner_in, raw_corner))
        )
    ]

    @pl.when(step == 0)
    def _():
        piece(0).start()
        for copy in others:
            copy.start()
        for k in range(1, tile // rows):
            piece(k).start()
        moved[:, :, 0:SPILL, :] = jnp.zeros((PLANES, blocks, SPILL, LANES), F32)
        moved_left[:, 0:SPILL, :] = jnp.zeros((PLANES, SPILL, LANES), F32)
        moved_up[:, :, SPILL:, :] = jnp.zeros((PLANES, blocks, SPILL, LANES), F32)
        moved_corner[:, SPILL:, :] = jnp.zeros((PLANES, SPILL, LANES), F32)
        for copy in others:
            copy.wait()

    piece(step).wait()
    first = pl.multiple_of(step * rows, rows)

    def shifted(load, shift, store):
        before = None
        for v in range(blocks):
            now = pltpu.roll(load(v).astype(F32), shift, 1)
            store(v, now if before is None else jnp.where(lanes < shift, before, now))
            before = now

    dy, dx, low, high = settings(row, col)
    here = pl.ds(first, rows)
    there = pl.ds(pl.multiple_of(first + SPILL, SPILL), rows)
    for p in range(PLANES):

        def store(v, x):
            moved[p, v, there, :] = x

        shifted(lambda v: raw[p, here, v * LANES : (v + 1) * LANES], dx, store)

    i = lines + (first - dy)
    row_fade = fade(i, (i >= jnp.maximum(low, 0)) & (i < high), tile)
    source = pl.ds(first + SPILL - dy, rows)
    for v in range(blocks):
        j = lanes + (v * LANES - dx)
        weight = row_fade * fade(j, j >= 0, tile)
        weights[:, v * LANES : (v + 1) * LANES] = weight
        for p in range(PLANES):
            x = moved[p, v, source, :]
            gain, level = terms[0, p : p + 1, :], terms[0, 2 + p : 3 + p, :]
            blended[p, :, v * LANES : (v + 1) * LANES] = (gain * x + level) * weight

    dy, dx, low, high = settings(row, left)
    for p in range(PLANES):
        moved_left[p, there, :] = pltpu.roll(raw_left[p, here, :].astype(F32), dx, 1)
    i = lines + (first - dy)
    j = lanes + (tile - dx)
    weight = fade(i, (i >= jnp.maximum(low, 0)) & (i < high) & (col > 0), tile)
    weight = weight * fade(j, j < tile, tile)
    source = pl.ds(first + SPILL - dy, rows)
    weights[:, 0:LANES] += weight
    for p in range(PLANES):
        x = moved_left[p, source, :]
        gain, level = terms[1, p : p + 1, :], terms[1, 2 + p : 3 + p, :]
        blended[p, :, 0:LANES] += (gain * x + level) * weight

    @pl.when((step == 0) & (row > 0))
    def _():
        dy, dx, low, high = settings(up, col)
        for p in range(PLANES):

            def store(v, x):
                moved_up[p, v, 0:SPILL, :] = x

            shifted(lambda v: raw_up[p, :, v * LANES : (v + 1) * LANES], dx, store)
        i = lines + (tile - dy)
        row_fade = fade(i, (i >= low) & (i < jnp.minimum(high, tile)), tile)
        source = pl.ds(SPILL - dy, rows)
        for v in range(blocks):
            j = lanes + (v * LANES - dx)
            weight = row_fade * fade(j, j >= 0, tile)
            weights[:, v * LANES : (v + 1) * LANES] += weight
            for p in range(PLANES):
                x = moved_up[p, v, source, :]
                gain, level = terms[2, p : p + 1, :], terms[2, 2 + p : 3 + p, :]
                blended[p, :, v * LANES : (v + 1) * LANES] += (gain * x + level) * weight

        @pl.when(col > 0)
        def _():
            dy, dx, low, high = settings(up, left)
            for p in range(PLANES):
                moved_corner[p, 0:SPILL, :] = pltpu.roll(raw_corner[p].astype(F32), dx, 1)
            i = lines + (tile - dy)
            j = lanes + (tile - dx)
            weight = fade(i, (i >= low) & (i < jnp.minimum(high, tile)), tile)
            weight = weight * fade(j, j < tile, tile)
            source = pl.ds(SPILL - dy, rows)
            weights[:, 0:LANES] += weight
            for p in range(PLANES):
                x = moved_corner[p, source, :]
                gain, level = terms[3, p : p + 1, :], terms[3, 2 + p : 3 + p, :]
                blended[p, :, 0:LANES] += (gain * x + level) * weight


def blend(tiles, offsets, bands, left_in, up_in, corner_in, terms):
    planes, tile, _ = tiles.shape
    dtype = tiles.dtype
    rows = BLOCK
    blocks = tile // LANES
    any_space = pl.BlockSpec(memory_space=pl.ANY)
    small = pl.BlockSpec(memory_space=pltpu.SMEM)
    places = jnp.stack([lax.axis_index("row"), lax.axis_index("col")]).astype(jnp.int32)
    return pl.pallas_call(
        blend_kernel,
        name="blend",
        grid=(tile // rows,),
        out_shape=(
            jax.ShapeDtypeStruct((planes, tile, tile), F32),
            jax.ShapeDtypeStruct((tile, tile), F32),
        ),
        in_specs=[small, small, small, any_space, any_space, any_space, any_space,
                  pl.BlockSpec(memory_space=pltpu.VMEM)],
        out_specs=(
            pl.BlockSpec((planes, rows, tile), lambda i: (0, i, 0)),
            pl.BlockSpec((rows, tile), lambda i: (i, 0)),
        ),
        scratch_shapes=[
            pltpu.VMEM((planes, tile, tile), dtype),
            pltpu.VMEM((planes, tile, STRIP), dtype),
            pltpu.VMEM((planes, STRIP, tile), dtype),
            pltpu.VMEM((planes, STRIP, STRIP), dtype),
            pltpu.VMEM((planes, blocks, SPILL + tile, LANES), F32),
            pltpu.VMEM((planes, SPILL + tile, LANES), F32),
            pltpu.VMEM((planes, blocks, 2 * SPILL, LANES), F32),
            pltpu.VMEM((planes, 2 * SPILL, LANES), F32),
            pltpu.SemaphoreType.DMA((tile // rows + 3,)),
        ],
        compiler_params=pltpu.CompilerParams(vmem_limit_bytes=48 * 1024 * 1024),
    )(places, offsets, bands, tiles, left_in, up_in, corner_in, terms)


def local(tiles, extents, offsets, bands):
    left_in, up_in, corner_in, terms = exchange(tiles, extents)
    return blend(tiles, offsets, bands, left_in, up_in, corner_in, terms)


def solution(mesh):
    return jax.shard_map(
        local,
        mesh=mesh,
        in_specs=(P(None, "row", "col"), P(), P(), P()),
        out_specs=(P(None, "row", "col"), P("row", "col")),
        check_vma=False,
    )
```

time: 157 us -> 47.9 us (0.31)
  the two profiles are of different devices: /device:TPU:28 before, /device:TPU:1 now
where the time goes in v1:
time: 47.9 us; the launch traced here: 47.7 us
  Pallas kernels  44.1 us (92%)
  local copies, waits for them, and re-layouts  2.9 us (6%)
  between operations  0.69 us (1%)
    pallas_call x1, Pallas kernels, exchange(): pl.pallas_call(exchange_kernel, name='exchange', out_shape=(jax.ShapeDtyp...  34.7 us
    pallas_call x1, Pallas kernels, blend(): pl.pallas_call(blend_kernel, name='blend', grid=(tile // rows,), out_shap...  9.39 us
    unnamed x10, local copies, waits for them, and re-layouts  2.9 us

profile of v1, /device:TPU:1, one launch (start us, length us, event | category | flops | bytes accessed | tf_op | source)
XLA Modules:
  0.0 47.7 jit_solution(9769339471050577852)
XLA Ops:
  0.6 0.0 copy-start.4
  0.6 0.0 copy-start.3
  0.7 0.1 pad_add_fusion.places
  0.7 0.0 copy-start
  0.7 2.2 %copy-done = bf16[2,1024,1024]{2,1,0:T(8,128)(2,1)S(1)} copy-done((bf16[2,1024,1024]{2,1,0:T(8,128)(2,1)S(1)}, bf16[2,1024,1024]{2,1,0:T(8,128)(2,1)}, u32[]{:S(2)}) %copy-start) | copy-done | bytes 4194328
  2.9 0.0 copy-start.2
  2.9 0.7 %copy-done.2 = s32[2,8,16]{2,1,0:T(8,128)S(1)} copy-done((s32[2,8,16]{2,1,0:T(8,128)S(1)}, s32[2,8,16]{2,1,0:T(8,128)}, u32[]{:S(2)}) %copy-start.2) | copy-done | bytes 1048
  3.6 0.0 copy-start.1
  3.6 34.7 %exchange.1 = (bf16[2,1024,128]{2,1,0:T(8,128)(2,1)S(1)}, bf16[2,128,1024]{2,1,0:T(8,128)(2,1)S(1)}, bf16[2,128,128]{2,1,0:T(8,128)(2,1)S(1)}, f32[4,4,128]{2,1,0:T(4,128)S(1)}) custom-call(s32[2,8,16]{2,1,0:T(8,128)S(1)} %copy-done.2, bf16[2,1024,1024]{2,1,0:T(8,128)(2,1)S(1)} %copy-done), custom_call_target="tpu_custom_call" | custom-call | tf_op jit(solution)/shard_map/exchange/pallas_call | solution.py:290
  38.3 0.0 copy-done.4
  38.3 0.0 copy-done.3
  38.3 0.0 copy-done.1
  38.3 9.4 %blend.1 = (f32[2,1024,1024]{2,1,0:T(8,128)}, f32[1024,1024]{1,0:T(8,128)}) custom-call(s32[2]{0:T(128)S(1)} %pad_add_fusion.places, s32[2,8,16]{2,1,0:T(8,128)S(1)} %copy-done.3, s32[2,8,16]{2,1,0:T(8,128)S(1)} %copy-done.4, bf16[2,1024,1024]{2,1,0:T(8,128)(2,1)S(1)} %copy-done.1, bf16[2,1024,128]{2,1,0:T(8,128)(2,1)S(1)} %get-tuple-element.6.left_in, ...), custom_call_target="tpu_custom_call" | custom-call | tf_op jit(solution)/shard_map/blend/pallas_call | solution.py:452
Async XLA Ops:
  0.6 37.7 %copy-start.4 = (s32[2,8,16]{2,1,0:T(8,128)S(1)}, s32[2,8,16]{2,1,0:T(8,128)}, u32[]{:S(2)}) copy-start(s32[2,8,16]{2,1,0:T(8,128)} %bands.1) | copy-start | bytes 3076
  0.6 37.7 %copy-start.3 = (s32[2,8,16]{2,1,0:T(8,128)S(1)}, s32[2,8,16]{2,1,0:T(8,128)}, u32[]{:S(2)}) copy-start(s32[2,8,16]{2,1,0:T(8,128)} %offsets.1) | copy-start | bytes 3076
  0.7 2.2 %copy-start = (bf16[2,1024,1024]{2,1,0:T(8,128)(2,1)S(1)}, bf16[2,1024,1024]{2,1,0:T(8,128)(2,1)}, u32[]{:S(2)}) copy-start(bf16[2,1024,1024]{2,1,0:T(8,128)(2,1)} %tiles.3) | copy-start | bytes 12582916
  2.9 0.7 %copy-start.2 = (s32[2,8,16]{2,1,0:T(8,128)S(1)}, s32[2,8,16]{2,1,0:T(8,128)}, u32[]{:S(2)}) copy-start(s32[2,8,16]{2,1,0:T(8,128)} %extents.1) | copy-start | bytes 3076
  3.6 34.7 %copy-start.1 = (bf16[2,1024,1024]{2,1,0:T(8,128)(2,1)S(1)}, bf16[2,1024,1024]{2,1,0:T(8,128)(2,1)}, u32[]{:S(2)}) copy-start(bf16[2,1024,1024]{2,1,0:T(8,128)(2,1)} %tiles.3) | copy-start | bytes 12582916

commit v2 on v1

v2 whole, which is shorter than its diff:
```python
import jax
import jax.numpy as jnp
from jax import lax
from jax.experimental import pallas as pl
from jax.experimental.pallas import tpu as pltpu
from jax.sharding import PartitionSpec as P

STRIP = 128
SPILL = 128
BLOCK = 128
LANES = 128
PLANES = 2
EPS = 1e-6
MESH = pl.DeviceIdType.MESH
F32 = jnp.float32

CENTRE = 36
BLENDED = ((0, 0), (0, -1), (-1, 0), (-1, -1))
SOURCES = tuple(
    (r, c)
    for r in range(-3, 3)
    for c in range(-3, 3)
    if min(abs(r - a) + abs(c - b) for a, b in BLENDED) <= 2 and (r, c) != (0, 0)
)
RIGHT_1, LEFT_1, DOWN_1, UP_1, RIGHT_2, DOWN_2, CORNER = range(7)


def slot_of(r, c):
    return CENTRE + 8 * r + c


def total(x):
    return jnp.sum(x, keepdims=True)


def fold(x):
    return jnp.sum(x.reshape(x.shape[0] // 8, 8, x.shape[1]), axis=0)


def sum_tall(ref, plane, first, mask, term):
    size = 128

    def body(i, acc):
        part = pl.ds(pl.multiple_of(i * size, size), size)
        x = ref[plane, part, first : first + STRIP].astype(F32)
        return acc + fold(term(x))

    acc = lax.fori_loop(0, ref.shape[1] // size, body, jnp.zeros((8, LANES), F32))
    return total(jnp.where(mask, acc, 0.0))


def sum_wide(ref, plane, first, extent, term):
    size = 16
    ids = lax.broadcasted_iota(jnp.int32, (size, LANES), 0)

    def body(i, acc):
        x = ref[plane, pl.ds(pl.multiple_of(first + i * size, size), size), :].astype(F32)
        t = term(x)
        part = sum(t[:, k : k + LANES] for k in range(0, x.shape[1], LANES))
        return acc + fold(jnp.where(ids + i * size < extent, part, 0.0))

    return total(lax.fori_loop(0, STRIP // size, body, jnp.zeros((8, LANES), F32)))


def cov_tall(own, row, col, other, other_row, count, means, plane, mask):
    size = 128

    def body(i, acc):
        start = pl.multiple_of(i * size, size)
        x = own[plane, pl.ds(row + start, size), col : col + STRIP].astype(F32) - means[0]
        y = other[plane, pl.ds(other_row + start, size), :].astype(F32) - means[1]
        return acc + fold(x * y)

    acc = lax.fori_loop(0, count // size, body, jnp.zeros((8, LANES), F32))
    return total(jnp.where(mask, acc, 0.0))


def cov_wide(own, row, col, other, other_col, count, means, plane, extent):
    size = 16
    ids = lax.broadcasted_iota(jnp.int32, (size, LANES), 0)

    def body(i, acc):
        start = pl.multiple_of(i * size, size)
        x = own[plane, pl.ds(row + start, size), col : col + count].astype(F32) - means[0]
        y = other[plane, pl.ds(start, size), other_col : other_col + count].astype(F32) - means[1]
        t = x * y
        part = sum(t[:, k : k + LANES] for k in range(0, count, LANES))
        return acc + fold(jnp.where(ids + i * size < extent, part, 0.0))

    return total(lax.fori_loop(0, STRIP // size, body, jnp.zeros((8, LANES), F32)))


def pair_terms(mean_a, var_a, mean_b, var_b, cov, valid):
    weight = cov * cov / ((var_a + EPS) * (var_b + EPS))
    ratio = 0.25 * (jnp.log(var_b + EPS) - jnp.log(var_a + EPS))
    shift = 0.5 * (mean_b - mean_a)
    return tuple(jnp.where(valid, t, 0.0) for t in (weight, weight * ratio, weight * shift))


def ahead(x, distance):
    return pltpu.roll(x, (LANES - distance) % LANES, 1)


def tile_terms(means, variances, covs, valid):
    across = pair_terms(means[0], variances[0], ahead(means[1], 1), ahead(variances[1], 1), covs[0], valid[0])
    along = pair_terms(means[2], variances[2], ahead(means[3], 8), ahead(variances[3], 8), covs[1], valid[1])
    back = [ahead(t, -1) for t in across]
    above = [ahead(t, -8) for t in along]
    scale = 1.0 + across[0] + along[0] + back[0] + above[0]
    return tuple((across[k] + along[k] - back[k] - above[k]) / scale for k in (1, 2))


def exchange_kernel(
    extents_in, offsets_in, tiles, shifted, left_in, up_in, corner_in, terms,
    extents, offsets, raw, half_r, half_d, moved, stats_out, stats_in, sums_out, sums_in,
    load_sem, send_sem, recv_sem, mean_send, mean_recv, sums_send, sums_recv,
):
    n_col, n_row = lax.axis_size("col"), lax.axis_size("row")
    col, row = lax.axis_index("col"), lax.axis_index("row")
    tile = raw.shape[1]
    half = tile // 2
    edge = tile - STRIP
    blocks = tile // LANES
    four = ((0, 1), (0, -1), (1, 0), (-1, 0))

    def exists(r, c):
        return (row + r >= 0) & (row + r < n_row) & (col + c >= 0) & (col + c < n_col)

    def place(r, c):
        return {"row": row + r, "col": col + c}

    sums_in[...] = jnp.zeros_like(sums_in)
    stats_in[...] = jnp.zeros_like(stats_in)

    barrier = pltpu.get_barrier_semaphore()
    expected = 0
    for r, c in SOURCES:

        @pl.when(exists(r, c))
        def _(r=r, c=c):
            pl.semaphore_signal(barrier, inc=1, device_id=place(r, c), device_id_type=MESH)

        expected = expected + exists(-r, -c).astype(jnp.int32)

    settings = [
        pltpu.make_async_copy(extents_in, extents, load_sem.at[blocks]),
        pltpu.make_async_copy(offsets_in, offsets, load_sem.at[blocks + 1]),
    ]
    for copy in settings:
        copy.start()
    loads = []
    for k in range(blocks):
        part = pl.ds(k * BLOCK, BLOCK)
        loads.append(pltpu.make_async_copy(tiles.at[:, part, :], raw.at[:, part, :], load_sem.at[k]))
        loads[k].start()

    pl.semaphore_wait(barrier, expected)

    class Remote:
        def __init__(self, src, dst, send, recv, r, c):
            self.there, self.here = exists(r, c), exists(-r, -c)
            self.copy = pltpu.make_async_remote_copy(
                src_ref=src,
                dst_ref=dst,
                send_sem=send,
                recv_sem=recv,
                device_id=place(r, c),
                device_id_type=MESH,
            )

        def start(self):
            pl.when(self.there)(self.copy.start)

        def wait_recv(self):
            pl.when(self.here)(self.copy.wait_recv)

        def wait_send(self):
            pl.when(self.there)(self.copy.wait_send)

    def bulk(index, src, dst, r, c):
        copy = Remote(src, dst, send_sem.at[index], recv_sem.at[index], r, c)
        copy.start()
        return copy

    first = [
        bulk(RIGHT_1, tiles.at[:, half:, edge:], left_in.at[:, half:, :], 0, 1),
        bulk(LEFT_1, tiles.at[:, :half, :STRIP], half_r, 0, -1),
        bulk(DOWN_1, tiles.at[:, edge:, half:], up_in.at[:, :, half:], 1, 0),
        bulk(UP_1, tiles.at[:, :STRIP, :half], half_d, -1, 0),
    ]

    for copy in settings:
        copy.wait()
    ext = (
        extents[0, row, col],
        extents[0, row, jnp.maximum(col - 1, 0)],
        extents[1, row, col],
        extents[1, jnp.maximum(row - 1, 0), col],
    )
    lanes = lax.broadcasted_iota(jnp.int32, (8, LANES), 1)
    windows = (lanes < ext[0], lanes < ext[1], ext[2], ext[3])
    numbers = [(e * tile).astype(F32) for e in ext]
    one = lax.broadcasted_iota(jnp.int32, (1, LANES), 1)

    for load in loads:
        load.wait()

    means = []
    packed = jnp.zeros((1, LANES), F32)
    for side in range(4):
        reduce = sum_tall if side < 2 else sum_wide
        begin = edge if side in (0, 2) else 0
        own_means = []
        for p in range(PLANES):
            mean = reduce(raw, p, begin, windows[side], lambda x: x) / numbers[side]

            def square(x, mean=mean):
                return (x - mean) * (x - mean)

            var = reduce(raw, p, begin, windows[side], square) / numbers[side]
            packed = jnp.where(one == 64 * p + 3 * side, mean, packed)
            packed = jnp.where(one == 64 * p + 3 * side + 1, var, packed)
            own_means.append(mean)
        means.append(own_means)
    stats_out[...] = packed
    opposite = (1, 0, 3, 2)
    early = []
    for side, (r, c) in enumerate(four):
        early.append(
            Remote(stats_out, stats_in.at[opposite[side]], mean_send.at[side], mean_recv.at[opposite[side]], r, c)
        )
        early[side].start()

    dy, dx = offsets[0, row, col], offsets[1, row, col]
    wide = lax.broadcasted_iota(jnp.int32, (BLOCK, LANES), 1)

    def shift_plane(p):
        moved[:, 0:SPILL, :] = jnp.zeros((blocks, SPILL, LANES), F32)

        def sideways(k, carry):
            start = pl.multiple_of(k * BLOCK, BLOCK)
            before = None
            for v in range(blocks):
                x = raw[p, pl.ds(start, BLOCK), v * LANES : (v + 1) * LANES].astype(F32)
                now = pltpu.roll(x, dx, 1)
                out = now if before is None else jnp.where(wide < dx, before, now)
                moved[v, pl.ds(start + SPILL, BLOCK), :] = out
                before = now
            return carry

        lax.fori_loop(0, blocks, sideways, 0)

        def downwards(k, carry):
            start = pl.multiple_of(k * BLOCK, BLOCK)
            for v in range(blocks):
                x = moved[v, pl.ds(start + SPILL - dy, BLOCK), :]
                shifted[p, pl.ds(start, BLOCK), v * LANES : (v + 1) * LANES] = x.astype(shifted.dtype)
            return carry

        lax.fori_loop(0, blocks, downwards, 0)

    shift_plane(0)

    for copy in early:
        copy.wait_recv()

    first[0].wait_recv()
    first[1].wait_recv()
    first[2].wait_recv()
    first[3].wait_recv()
    for side in range(4):
        far = stats_in[side]
        for p in range(PLANES):
            k = 64 * p + 3 * opposite[side]
            pair = (means[side][p], far[:, k : k + 1])
            if side == 0:
                cov = cov_tall(raw, 0, edge, half_r, 0, half, pair, p, windows[side])
            elif side == 1:
                cov = cov_tall(raw, half, 0, left_in, half, half, pair, p, windows[side])
            elif side == 2:
                cov = cov_wide(raw, edge, 0, half_d, 0, half, pair, p, windows[side])
            else:
                cov = cov_wide(raw, 0, half, up_in, half, half, pair, p, windows[side])
            packed = jnp.where(one == 64 * p + 3 * side + 2, cov / numbers[side], packed)
    sums_out[...] = packed
    sums_in[CENTRE] = packed
    spread = []
    for k, (r, c) in enumerate(SOURCES):
        copy = Remote(sums_out, sums_in.at[slot_of(r, c)], sums_send.at[k], sums_recv.at[k], -r, -c)
        copy.start()
        spread.append(copy)

    second = [
        bulk(RIGHT_2, tiles.at[:, :half, edge:], left_in.at[:, :half, :], 0, 1),
        bulk(DOWN_2, tiles.at[:, edge:, :half], up_in.at[:, :, :half], 1, 0),
        bulk(CORNER, left_in.at[:, edge:, :], corner_in, 1, 0),
    ]

    shift_plane(1)

    for copy in spread:
        copy.wait_recv()

    table = jnp.transpose(sums_in[:, 0, :])

    def quantity(k):
        return jnp.concatenate([table[k : k + 1, :], table[64 + k : 65 + k, :]], axis=0)

    slot = lax.broadcasted_iota(jnp.int32, (PLANES, LANES), 1)
    slot_row = row + lax.shift_right_logical(slot, 3) - 4
    slot_col = col + (slot & 7) - 4
    inside = (slot_row >= 0) & (slot_row < n_row) & (slot_col >= 0) & (slot_col < n_col)
    valid = (inside & (slot_col < n_col - 1), inside & (slot_row < n_row - 1))
    sides = [quantity(3 * side) for side in range(4)]
    spreads = [quantity(3 * side + 1) for side in range(4)]
    covs = (quantity(2) + ahead(quantity(5), 1), quantity(8) + ahead(quantity(11), 8))
    gain_one, level_one = tile_terms(sides, spreads, covs, valid)
    scale = jnp.exp(gain_one)
    gain_two, level_two = tile_terms(
        [scale * m + level_one for m in sides],
        [scale * (scale * v) for v in spreads],
        (scale * (ahead(scale, 1) * covs[0]), scale * (ahead(scale, 8) * covs[1])),
        valid,
    )
    gain = jnp.exp(gain_one + gain_two)
    level = jnp.exp(gain_two) * level_one + level_two
    for k, (r, c) in enumerate(BLENDED):
        s = slot_of(r, c)
        terms[k, 0:2, :] = jnp.broadcast_to(gain[:, s : s + 1], (PLANES, LANES))
        terms[k, 2:4, :] = jnp.broadcast_to(level[:, s : s + 1], (PLANES, LANES))
    for copy in second:
        copy.wait_recv()
    for copy in (*early, *first, *spread, *second):
        copy.wait_send()


def exchange(tiles, extents, offsets):
    planes, tile, _ = tiles.shape
    dtype = tiles.dtype
    half = tile // 2
    blocks = tile // LANES
    in_vmem = pl.BlockSpec(memory_space=pltpu.VMEM)
    one = pltpu.VMEM((1, LANES), F32)
    dma = pltpu.SemaphoreType.DMA
    return pl.pallas_call(
        exchange_kernel,
        name="exchange",
        out_shape=(
            jax.ShapeDtypeStruct((planes, tile, tile), dtype),
            jax.ShapeDtypeStruct((planes, tile, STRIP), dtype),
            jax.ShapeDtypeStruct((planes, STRIP, tile), dtype),
            jax.ShapeDtypeStruct((planes, STRIP, STRIP), dtype),
            jax.ShapeDtypeStruct((4, 4, LANES), F32),
        ),
        in_specs=[pl.BlockSpec(memory_space=pl.ANY)] * 3,
        out_specs=(in_vmem,) * 5,
        scratch_shapes=[
            pltpu.SMEM(extents.shape, extents.dtype),
            pltpu.SMEM(offsets.shape, offsets.dtype),
            pltpu.VMEM((planes, tile, tile), dtype),
            pltpu.VMEM((planes, half, STRIP), dtype),
            pltpu.VMEM((planes, STRIP, half), dtype),
            pltpu.VMEM((blocks, SPILL + tile, LANES), F32),
            one,
            pltpu.VMEM((4, 1, LANES), F32),
            one,
            pltpu.VMEM((LANES, 1, LANES), F32),
            dma((blocks + 2,)),
            dma((7,)),
            dma((7,)),
            dma((4,)),
            dma((4,)),
            dma((len(SOURCES),)),
            dma((len(SOURCES),)),
        ],
        compiler_params=pltpu.CompilerParams(
            collective_id=0, has_side_effects=True, vmem_limit_bytes=48 * 1024 * 1024
        ),
    )(extents, offsets, tiles)


def fade(ids, limit, tile):
    steps = jnp.minimum(ids, tile - 1 - ids) + 1
    return jnp.where(limit, steps.astype(F32) * (2.0 / tile), 0.0)


def blend_kernel(
    places, offsets, bands, shifted, raw_left, raw_up, raw_corner, terms, blended, weights,
    moved_left, moved_up, moved_corner,
):
    step = pl.program_id(0)
    rows = weights.shape[0]
    tile = weights.shape[1]
    blocks = tile // LANES
    lanes = lax.broadcasted_iota(jnp.int32, (rows, LANES), 1)
    lines = lax.broadcasted_iota(jnp.int32, (rows, LANES), 0)
    row, col = places[0], places[1]
    up, left = jnp.maximum(row - 1, 0), jnp.maximum(col - 1, 0)
    block = lax.rem(step + 1, tile // rows)
    first = pl.multiple_of(block * rows, rows)
    here = pl.ds(first, rows)

    def settings(r, c):
        return offsets[0, r, c], offsets[1, r, c], bands[0, r, c] * BLOCK, bands[1, r, c] * BLOCK

    def corrected(x, k, p):
        return terms[k, p : p + 1, :] * x + terms[k, 2 + p : 3 + p, :]

    @pl.when(step == 0)
    def _():
        moved_left[:, 0:SPILL, :] = jnp.zeros((PLANES, SPILL, LANES), F32)
        dx = offsets[1, row, left]
        for k in range(blocks):
            for p in range(PLANES):
                x = raw_left[p, k * BLOCK : (k + 1) * BLOCK, :].astype(F32)
                moved_left[p, SPILL + k * BLOCK : SPILL + (k + 1) * BLOCK, :] = pltpu.roll(x, dx, 1)

    dy, dx, low, high = settings(row, col)
    i = lines + (first - dy)
    row_fade = fade(i, (i >= jnp.maximum(low, 0)) & (i < high), tile)
    for v in range(blocks):
        j = lanes + (v * LANES - dx)
        weight = row_fade * fade(j, j >= 0, tile)
        weights[:, v * LANES : (v + 1) * LANES] = weight
        for p in range(PLANES):
            x = shifted[p, here, v * LANES : (v + 1) * LANES].astype(F32)
            blended[p, :, v * LANES : (v + 1) * LANES] = corrected(x, 0, p) * weight

    @pl.when(col > 0)
    def _():
        dy, dx, low, high = settings(row, left)
        i = lines + (first - dy)
        j = lanes + (tile - dx)
        weight = fade(i, (i >= jnp.maximum(low, 0)) & (i < high), tile) * fade(j, j < tile, tile)
        source = pl.ds(first + SPILL - dy, rows)
        weights[:, 0:LANES] += weight
        for p in range(PLANES):
            blended[p, :, 0:LANES] += corrected(moved_left[p, source, :], 1, p) * weight

    @pl.when((block == 0) & (row > 0))
    def _():
        dy, dx, low, high = settings(up, col)
        for p in range(PLANES):
            before = None
            for v in range(blocks):
                now = pltpu.roll(raw_up[p, :, v * LANES : (v + 1) * LANES].astype(F32), dx, 1)
                moved_up[p, v, 0:SPILL, :] = now if before is None else jnp.where(lanes < dx, before, now)
                moved_up[p, v, SPILL:, :] = jnp.zeros((SPILL, LANES), F32)
                before = now
        i = lines + (tile - dy)
        row_fade = fade(i, (i >= low) & (i < jnp.minimum(high, tile)), tile)
        source = pl.ds(SPILL - dy, rows)
        for v in range(blocks):
            j = lanes + (v * LANES - dx)
            weight = row_fade * fade(j, j >= 0, tile)
            weights[:, v * LANES : (v + 1) * LANES] += weight
            for p in range(PLANES):
                x = moved_up[p, v, source, :]
                blended[p, :, v * LANES : (v + 1) * LANES] += corrected(x, 2, p) * weight

        @pl.when(col > 0)
        def _():
            dy, dx, low, high = settings(up, left)
            for p in range(PLANES):
                moved_corner[p, 0:SPILL, :] = pltpu.roll(raw_corner[p].astype(F32), dx, 1)
                moved_corner[p, SPILL:, :] = jnp.zeros((SPILL, LANES), F32)
            i = lines + (tile - dy)
            j = lanes + (tile - dx)
            weight = fade(i, (i >= low) & (i < jnp.minimum(high, tile)), tile) * fade(j, j < tile, tile)
            source = pl.ds(SPILL - dy, rows)
            weights[:, 0:LANES] += weight
            for p in range(PLANES):
                blended[p, :, 0:LANES] += corrected(moved_corner[p, source, :], 3, p) * weight


def blend(offsets, bands, shifted, left_in, up_in, corner_in, terms):
    planes, tile, _ = shifted.shape
    rows = BLOCK
    blocks = tile // LANES
    count = tile // rows
    in_vmem = pl.BlockSpec(memory_space=pltpu.VMEM)
    in_smem = pl.BlockSpec(memory_space=pltpu.SMEM)
    places = jnp.stack([lax.axis_index("row"), lax.axis_index("col")]).astype(jnp.int32)
    return pl.pallas_call(
        blend_kernel,
        name="blend",
        grid=(count,),
        out_shape=(
            jax.ShapeDtypeStruct((planes, tile, tile), F32),
            jax.ShapeDtypeStruct((tile, tile), F32),
        ),
        in_specs=[in_smem] * 3 + [in_vmem] * 5,
        out_specs=(
            pl.BlockSpec((planes, rows, tile), lambda i: (0, lax.rem(i + 1, count), 0)),
            pl.BlockSpec((rows, tile), lambda i: (lax.rem(i + 1, count), 0)),
        ),
        scratch_shapes=[
            pltpu.VMEM((planes, SPILL + tile, LANES), F32),
            pltpu.VMEM((planes, blocks, 2 * SPILL, LANES), F32),
            pltpu.VMEM((planes, 2 * SPILL, LANES), F32),
        ],
        compiler_params=pltpu.CompilerParams(vmem_limit_bytes=32 * 1024 * 1024),
    )(places, offsets, bands, shifted, left_in, up_in, corner_in, terms)


def local(tiles, extents, offsets, bands):
    shifted, left_in, up_in, corner_in, terms = exchange(tiles, extents, offsets)
    return blend(offsets, bands, shifted, left_in, up_in, corner_in, terms)


def solution(mesh):
    return jax.shard_map(
        local,
        mesh=mesh,
        in_specs=(P(None, "row", "col"), P(), P(), P()),
        out_specs=(P(None, "row", "col"), P("row", "col")),
        check_vma=False,
    )
```

time: 47.9 us -> 39 us (0.81)
  the two profiles are of different devices: /device:TPU:1 before, /device:TPU:26 now
where the time goes in v2:
time: 39 us; the launch traced here: 38.8 us
  Pallas kernels  36.7 us (94%)
  local copies, waits for them, and re-layouts  1.4 us (4%)
  between operations  0.66 us (2%)
    pallas_call x1, Pallas kernels, exchange(): pl.pallas_call(exchange_kernel, name='exchange', out_shape=(jax.ShapeDtyp...  28.4 us
    pallas_call x1, Pallas kernels, blend(): pl.pallas_call(blend_kernel, name='blend', grid=(count,), out_shape=(jax....  8.25 us
    unnamed x6, local copies, waits for them, and re-layouts  1.4 us

profile of v2, /device:TPU:26, one launch (start us, length us, event | category | flops | bytes accessed | tf_op | source)
XLA Modules:
  0.0 38.8 jit_solution(9047641970420369835)
XLA Ops:
  0.6 0.0 copy-start.2
  0.6 0.1 pad_add_fusion.places
  0.7 0.0 copy-start
  0.7 0.7 %copy-done = s32[2,8,16]{2,1,0:T(8,128)S(1)} copy-done((s32[2,8,16]{2,1,0:T(8,128)S(1)}, s32[2,8,16]{2,1,0:T(8,128)}, u32[]{:S(2)}) %copy-start) | copy-done | bytes 1048
  1.4 0.0 copy-start.1
  1.4 0.7 %copy-done.1 = s32[2,8,16]{2,1,0:T(8,128)S(1)} copy-done((s32[2,8,16]{2,1,0:T(8,128)S(1)}, s32[2,8,16]{2,1,0:T(8,128)}, u32[]{:S(2)}) %copy-start.1) | copy-done | bytes 1048
  2.1 28.4 %exchange.1 = (bf16[2,1024,1024]{2,1,0:T(8,128)(2,1)S(1)}, bf16[2,1024,128]{2,1,0:T(8,128)(2,1)S(1)}, bf16[2,128,1024]{2,1,0:T(8,128)(2,1)S(1)}, bf16[2,128,128]{2,1,0:T(8,128)(2,1)S(1)}, f32[4,4,128]{2,1,0:T(4,128)S(1)}) custom-call(s32[2,8,16]{2,1,0:T(8,128)S(1)} %copy-done.1, s32[2,8,16]{2,1,0:T(8,128)S(1)} %copy-done, bf16[2,1024,1024]{2,1,0:T(8,128)(2,1)} %tiles.1), custom_call_target="tpu_custom_call" | custom-call | tf_op jit(solution)/shard_map/exchange/pallas_call | solution.py:345
  30.6 0.0 copy-done.2
  30.6 8.3 %blend.1 = (f32[2,1024,1024]{2,1,0:T(8,128)}, f32[1024,1024]{1,0:T(8,128)}) custom-call(s32[2]{0:T(128)S(1)} %pad_add_fusion.places, s32[2,8,16]{2,1,0:T(8,128)S(1)} %copy-done, s32[2,8,16]{2,1,0:T(8,128)S(1)} %copy-done.2, bf16[2,1024,1024]{2,1,0:T(8,128)(2,1)S(1)} %get-tuple-element.7.shifted, bf16[2,1024,128]{2,1,0:T(8,128)(2,1)S(1)} %get-tuple-element.8.raw_left, ...), custom_call_target="tpu_custom_call" | custom-call | tf_op jit(solution)/shard_map/blend/pallas_call | solution.py:484
Async XLA Ops:
  0.6 29.9 %copy-start.2 = (s32[2,8,16]{2,1,0:T(8,128)S(1)}, s32[2,8,16]{2,1,0:T(8,128)}, u32[]{:S(2)}) copy-start(s32[2,8,16]{2,1,0:T(8,128)} %bands.1) | copy-start | bytes 3076
  0.7 0.7 %copy-start = (s32[2,8,16]{2,1,0:T(8,128)S(1)}, s32[2,8,16]{2,1,0:T(8,128)}, u32[]{:S(2)}) copy-start(s32[2,8,16]{2,1,0:T(8,128)} %offsets.1) | copy-start | bytes 3076
  1.4 0.7 %copy-start.1 = (s32[2,8,16]{2,1,0:T(8,128)S(1)}, s32[2,8,16]{2,1,0:T(8,128)}, u32[]{:S(2)}) copy-start(s32[2,8,16]{2,1,0:T(8,128)} %extents_in.1) | copy-start | bytes 3076

commit v3 on v2

v3 whole, which is shorter than its diff:
```python
import jax
import jax.numpy as jnp
from jax import lax
from jax.experimental import pallas as pl
from jax.experimental.pallas import tpu as pltpu
from jax.sharding import PartitionSpec as P

STRIP = 128
SPILL = 128
BLOCK = 128
LANES = 128
ROWS = 64
PLANES = 2
EPS = 1e-6
MESH = pl.DeviceIdType.MESH
F32 = jnp.float32

CENTRE = 36
BLENDED = ((0, 0), (0, -1), (-1, 0), (-1, -1))
SOURCES = tuple(
    (r, c)
    for r in range(-3, 3)
    for c in range(-3, 3)
    if min(abs(r - a) + abs(c - b) for a, b in BLENDED) <= 2 and (r, c) != (0, 0)
)
RIGHT_1, LEFT_1, DOWN_1, UP_1, RIGHT_2, DOWN_2, CORNER = range(7)


def slot_of(r, c):
    return CENTRE + 8 * r + c


def total(x):
    return jnp.sum(x, keepdims=True)


def fold(x):
    return jnp.sum(x.reshape(x.shape[0] // 8, 8, x.shape[1]), axis=0)


def sum_tall(ref, plane, first, mask, term):
    size = 128

    def body(i, acc):
        part = pl.ds(pl.multiple_of(i * size, size), size)
        x = ref[plane, part, first : first + STRIP].astype(F32)
        return acc + fold(term(x))

    acc = lax.fori_loop(0, ref.shape[1] // size, body, jnp.zeros((8, LANES), F32))
    return total(jnp.where(mask, acc, 0.0))


def sum_wide(ref, plane, first, extent, term):
    size = 16
    ids = lax.broadcasted_iota(jnp.int32, (size, LANES), 0)

    def body(i, acc):
        x = ref[plane, pl.ds(pl.multiple_of(first + i * size, size), size), :].astype(F32)
        t = term(x)
        part = sum(t[:, k : k + LANES] for k in range(0, x.shape[1], LANES))
        return acc + fold(jnp.where(ids + i * size < extent, part, 0.0))

    return total(lax.fori_loop(0, STRIP // size, body, jnp.zeros((8, LANES), F32)))


def cov_tall(own, row, col, other, other_row, count, means, plane, mask):
    size = 128
    acc = jnp.zeros((8, LANES), F32)
    for start in range(0, count, size):
        x = own[plane, row + start : row + start + size, col : col + STRIP].astype(F32)
        y = other[plane, other_row + start : other_row + start + size, :].astype(F32)
        x = x.reshape(size // 8, 8, LANES) - means[0][None]
        y = y.reshape(size // 8, 8, LANES) - means[1][None]
        acc = acc + jnp.sum(x * y, axis=0)
    return jnp.sum(jnp.where(mask, acc, 0.0), axis=0, keepdims=True)


def cov_wide(own, row, col, other, other_col, count, means, plane, extent):
    size = 16
    ids = lax.broadcasted_iota(jnp.int32, (8, LANES), 0)
    acc = jnp.zeros((8, LANES), F32)
    for start in range(0, STRIP, size):
        part = jnp.zeros((size // 8, 8, LANES), F32)
        for k in range(0, count, LANES):
            x = own[plane, row + start : row + start + size, col + k : col + k + LANES].astype(F32)
            y = other[plane, start : start + size, other_col + k : other_col + k + LANES].astype(F32)
            x = x.reshape(size // 8, 8, LANES) - means[0][None]
            y = y.reshape(size // 8, 8, LANES) - means[1][None]
            part = part + x * y
        for k in range(size // 8):
            acc = acc + jnp.where(ids + (start + 8 * k) < extent, part[k], 0.0)
    return jnp.sum(acc, axis=0, keepdims=True)


def pair_terms(mean_a, var_a, mean_b, var_b, cov, valid):
    weight = cov * cov / ((var_a + EPS) * (var_b + EPS))
    ratio = 0.25 * (jnp.log(var_b + EPS) - jnp.log(var_a + EPS))
    shift = 0.5 * (mean_b - mean_a)
    return tuple(jnp.where(valid, t, 0.0) for t in (weight, weight * ratio, weight * shift))


def ahead(x, distance):
    return pltpu.roll(x, (LANES - distance) % LANES, 1)


def tile_terms(means, variances, covs, valid):
    across = pair_terms(means[0], variances[0], ahead(means[1], 1), ahead(variances[1], 1), covs[0], valid[0])
    along = pair_terms(means[2], variances[2], ahead(means[3], 8), ahead(variances[3], 8), covs[1], valid[1])
    back = [ahead(t, -1) for t in across]
    above = [ahead(t, -8) for t in along]
    scale = 1.0 + across[0] + along[0] + back[0] + above[0]
    return tuple((across[k] + along[k] - back[k] - above[k]) / scale for k in (1, 2))


def exchange_kernel(
    settings_in, tiles, shifted, left_in, up_in, corner_in, terms, places,
    settings, raw, half_r, half_d, moved, stats_out, stats_in, sums_out, sums_in,
    load_sem, send_sem, recv_sem, mean_send, mean_recv, sums_send, sums_recv,
):
    n_col, n_row = lax.axis_size("col"), lax.axis_size("row")
    col, row = lax.axis_index("col"), lax.axis_index("row")
    tile = raw.shape[1]
    half = tile // 2
    edge = tile - STRIP
    blocks = tile // LANES
    four = ((0, 1), (0, -1), (1, 0), (-1, 0))

    def exists(r, c):
        return (row + r >= 0) & (row + r < n_row) & (col + c >= 0) & (col + c < n_col)

    def place(r, c):
        return {"row": row + r, "col": col + c}

    sums_in[...] = jnp.zeros_like(sums_in)
    stats_in[...] = jnp.zeros_like(stats_in)

    barrier = pltpu.get_barrier_semaphore()
    expected = 0
    for r, c in SOURCES:

        @pl.when(exists(r, c))
        def _(r=r, c=c):
            pl.semaphore_signal(barrier, inc=1, device_id=place(r, c), device_id_type=MESH)

        expected = expected + exists(-r, -c).astype(jnp.int32)

    fetch = pltpu.make_async_copy(settings_in, settings, load_sem.at[blocks])
    fetch.start()
    loads = []
    for k in range(blocks):
        part = pl.ds(k * BLOCK, BLOCK)
        loads.append(pltpu.make_async_copy(tiles.at[:, part, :], raw.at[:, part, :], load_sem.at[k]))
        loads[k].start()

    pl.semaphore_wait(barrier, expected)

    class Remote:
        def __init__(self, src, dst, send, recv, r, c, wanted=True):
            self.there, self.here = exists(r, c) & wanted, exists(-r, -c) & wanted
            self.copy = pltpu.make_async_remote_copy(
                src_ref=src,
                dst_ref=dst,
                send_sem=send,
                recv_sem=recv,
                device_id=place(r, c),
                device_id_type=MESH,
            )

        def start(self):
            pl.when(self.there)(self.copy.start)

        def wait_recv(self):
            pl.when(self.here)(self.copy.wait_recv)

        def wait_send(self):
            pl.when(self.there)(self.copy.wait_send)

    def bulk(index, src, dst, r, c, wanted=True):
        copy = Remote(src, dst, send_sem.at[index], recv_sem.at[index], r, c, wanted)
        copy.start()
        return copy

    first = [
        bulk(RIGHT_1, tiles.at[:, half:, edge:], left_in.at[:, half:, :], 0, 1),
        bulk(LEFT_1, tiles.at[:, :half, :STRIP], half_r, 0, -1),
        bulk(DOWN_1, tiles.at[:, edge:, half:], up_in.at[:, :, half:], 1, 0),
        bulk(UP_1, tiles.at[:, :STRIP, :half], half_d, -1, 0),
    ]

    fetch.wait()
    ext = (
        settings[0, row, col],
        settings[0, row, jnp.maximum(col - 1, 0)],
        settings[1, row, col],
        settings[1, jnp.maximum(row - 1, 0), col],
    )
    lanes = lax.broadcasted_iota(jnp.int32, (8, LANES), 1)
    windows = (lanes < ext[0], lanes < ext[1], ext[2], ext[3])
    numbers = [(e * tile).astype(F32) for e in ext]
    one = lax.broadcasted_iota(jnp.int32, (1, LANES), 1)

    for load in loads:
        load.wait()

    means = []
    packed = jnp.zeros((1, LANES), F32)
    count_row = jnp.ones((1, LANES), F32)
    for side in range(4):
        reduce = sum_tall if side < 2 else sum_wide
        begin = edge if side in (0, 2) else 0
        own_means = []
        for p in range(PLANES):
            mean = reduce(raw, p, begin, windows[side], lambda x: x) / numbers[side]

            def square(x, mean=mean):
                return (x - mean) * (x - mean)

            var = reduce(raw, p, begin, windows[side], square) / numbers[side]
            packed = jnp.where(one == 64 * p + 3 * side, mean, packed)
            packed = jnp.where(one == 64 * p + 3 * side + 1, var, packed)
            count_row = jnp.where(one == 64 * p + 3 * side + 2, numbers[side], count_row)
            own_means.append(mean)
        means.append(own_means)
    stats_out[...] = packed
    opposite = (1, 0, 3, 2)
    early = []
    for side, (r, c) in enumerate(four):
        early.append(
            Remote(stats_out, stats_in.at[opposite[side]], mean_send.at[side], mean_recv.at[opposite[side]], r, c)
        )
        early[side].start()

    second = [bulk(RIGHT_2, tiles.at[:, :half, edge:], left_in.at[:, :half, :], 0, 1)]
    second.append(bulk(DOWN_2, tiles.at[:, edge:, :half], up_in.at[:, :, :half], 1, 0))

    dy, dx = settings[2, row, col], settings[3, row, col]
    wide = lax.broadcasted_iota(jnp.int32, (BLOCK, LANES), 1)

    def shift_plane(p):
        moved[:, 0:SPILL, :] = jnp.zeros((blocks, SPILL, LANES), F32)

        def sideways(k, carry):
            start = pl.multiple_of(k * BLOCK, BLOCK)
            before = None
            for v in range(blocks):
                x = raw[p, pl.ds(start, BLOCK), v * LANES : (v + 1) * LANES].astype(F32)
                now = pltpu.roll(x, dx, 1)
                out = now if before is None else jnp.where(wide < dx, before, now)
                moved[v, pl.ds(start + SPILL, BLOCK), :] = out
                before = now
            return carry

        lax.fori_loop(0, blocks, sideways, 0)

        def downwards(k, carry):
            start = pl.multiple_of(k * BLOCK, BLOCK)
            for v in range(blocks):
                x = moved[v, pl.ds(start + SPILL - dy, BLOCK), :]
                shifted[p, pl.ds(start, BLOCK), v * LANES : (v + 1) * LANES] = x.astype(shifted.dtype)
            return carry

        lax.fori_loop(0, blocks, downwards, 0)

    for k, (r, c) in enumerate(BLENDED):
        tile_row, tile_col = jnp.maximum(row + r, 0), jnp.maximum(col + c, 0)
        low, high = settings[4, tile_row, tile_col] * BLOCK, settings[5, tile_row, tile_col] * BLOCK
        entries = (
            settings[2, tile_row, tile_col],
            settings[3, tile_row, tile_col],
            jnp.maximum(low, 0),
            jnp.where(exists(r, c), jnp.minimum(high, tile), 0),
        )
        for q, entry in enumerate(entries):
            places[4 * k + q : 4 * k + q + 1, :] = jnp.broadcast_to(entry, (1, LANES))

    for absent, ref in ((col == 0, left_in), (row == 0, up_in), ((row == 0) | (col == 0), corner_in)):

        @pl.when(absent)
        def _(ref=ref):
            ref[...] = jnp.zeros_like(ref)

    shift_plane(0)

    for copy in early:
        copy.wait_recv()

    def covariance(side):
        rows = []
        for p in range(PLANES):
            k = 64 * p + 3 * opposite[side]
            pair = (
                jnp.broadcast_to(means[side][p], (8, LANES)),
                jnp.broadcast_to(stats_in[side][:, k : k + 1], (8, LANES)),
            )
            if side == 0:
                rows.append(cov_tall(raw, 0, edge, half_r, 0, half, pair, p, windows[side]))
            elif side == 1:
                rows.append(cov_tall(raw, half, 0, left_in, half, half, pair, p, windows[side]))
            elif side == 2:
                rows.append(cov_wide(raw, edge, 0, half_d, 0, half, pair, p, windows[side]))
            else:
                rows.append(cov_wide(raw, 0, half, up_in, half, half, pair, p, windows[side]))
        return rows

    cov_rows = [None] * 4
    for side, copy in ((2, first[3]), (3, first[2])):
        copy.wait_recv()
        cov_rows[side] = covariance(side)
    for side, copy in ((0, first[1]), (1, first[0])):
        copy.wait_recv()
        cov_rows[side] = covariance(side)
    sums = jnp.sum(jnp.concatenate([r for rows in cov_rows for r in rows], axis=0), axis=1, keepdims=True)
    index = lax.broadcasted_iota(jnp.int32, (8, LANES), 0)
    chosen = lanes == 64 * (index & 1) + 3 * lax.shift_right_logical(index, 1) + 2
    cov = jnp.sum(jnp.where(chosen, sums, 0.0), axis=0, keepdims=True)
    packed = packed + cov / count_row
    sums_out[...] = packed
    sums_in[CENTRE] = packed
    spread = []
    for k, (r, c) in enumerate(SOURCES):
        copy = Remote(sums_out, sums_in.at[slot_of(r, c)], sums_send.at[k], sums_recv.at[k], -r, -c)
        copy.start()
        spread.append(copy)

    second.append(bulk(CORNER, left_in.at[:, edge:, :], corner_in, 1, 0, col > 0))

    shift_plane(1)

    for copy in spread:
        copy.wait_recv()

    table = sums_in[:, 0, :]
    table = jnp.transpose(jnp.concatenate([table, table], axis=0))

    def quantity(k):
        return jnp.concatenate([table[k : k + 1, :], table[64 + k : 65 + k, :]], axis=0)

    slot = lax.broadcasted_iota(jnp.int32, (PLANES, LANES), 1)
    slot_row = row + lax.shift_right_logical(slot, 3) - 4
    slot_col = col + (slot & 7) - 4
    inside = (slot_row >= 0) & (slot_row < n_row) & (slot_col >= 0) & (slot_col < n_col)
    valid = (inside & (slot_col < n_col - 1), inside & (slot_row < n_row - 1))
    sides = [quantity(3 * side) for side in range(4)]
    spreads = [quantity(3 * side + 1) for side in range(4)]
    covs = (quantity(2) + ahead(quantity(5), 1), quantity(8) + ahead(quantity(11), 8))
    gain_one, level_one = tile_terms(sides, spreads, covs, valid)
    scale = jnp.exp(gain_one)
    gain_two, level_two = tile_terms(
        [scale * m + level_one for m in sides],
        [scale * (scale * v) for v in spreads],
        (scale * (ahead(scale, 1) * covs[0]), scale * (ahead(scale, 8) * covs[1])),
        valid,
    )
    gain = jnp.exp(gain_one + gain_two)
    level = jnp.exp(gain_two) * level_one + level_two
    for k, (r, c) in enumerate(BLENDED):
        s = slot_of(r, c)
        terms[k, 0:2, :] = jnp.broadcast_to(gain[:, s : s + 1], (PLANES, LANES))
        terms[k, 2:4, :] = jnp.broadcast_to(level[:, s : s + 1], (PLANES, LANES))
    for copy in second:
        copy.wait_recv()
    for copy in (*early, *first, *spread, *second):
        copy.wait_send()


def exchange(tiles, settings):
    planes, tile, _ = tiles.shape
    dtype = tiles.dtype
    half = tile // 2
    blocks = tile // LANES
    in_vmem = pl.BlockSpec(memory_space=pltpu.VMEM)
    one = pltpu.VMEM((1, LANES), F32)
    dma = pltpu.SemaphoreType.DMA
    return pl.pallas_call(
        exchange_kernel,
        name="exchange",
        out_shape=(
            jax.ShapeDtypeStruct((planes, tile, tile), dtype),
            jax.ShapeDtypeStruct((planes, tile, STRIP), dtype),
            jax.ShapeDtypeStruct((planes, STRIP, tile), dtype),
            jax.ShapeDtypeStruct((planes, STRIP, STRIP), dtype),
            jax.ShapeDtypeStruct((4, 4, LANES), F32),
            jax.ShapeDtypeStruct((16, LANES), jnp.int32),
        ),
        in_specs=[pl.BlockSpec(memory_space=pl.ANY)] * 2,
        out_specs=(in_vmem,) * 6,
        scratch_shapes=[
            pltpu.SMEM(settings.shape, settings.dtype),
            pltpu.VMEM((planes, tile, tile), dtype),
            pltpu.VMEM((planes, half, STRIP), dtype),
            pltpu.VMEM((planes, STRIP, half), dtype),
            pltpu.VMEM((blocks, SPILL + tile, LANES), F32),
            one,
            pltpu.VMEM((4, 1, LANES), F32),
            one,
            pltpu.VMEM((64, 1, LANES), F32),
            dma((blocks + 1,)),
            dma((7,)),
            dma((7,)),
            dma((4,)),
            dma((4,)),
            dma((len(SOURCES),)),
            dma((len(SOURCES),)),
        ],
        compiler_params=pltpu.CompilerParams(
            collective_id=0, has_side_effects=True, vmem_limit_bytes=48 * 1024 * 1024
        ),
    )(settings, tiles)


def fade(ids, limit, tile):
    steps = jnp.minimum(ids, tile - 1 - ids) + 1
    return jnp.where(limit, steps.astype(F32) * (2.0 / tile), 0.0)


def blend_kernel(
    shifted, raw_left, raw_up, raw_corner, terms, places, blended, weights,
    out, out_weight, moved_left, moved_up, moved_corner, sem,
):
    tile = weights.shape[0]
    rows = ROWS
    count = tile // rows
    blocks = tile // LANES
    lanes = lax.broadcasted_iota(jnp.int32, (rows, LANES), 1)
    lines = lax.broadcasted_iota(jnp.int32, (rows, LANES), 0)
    top_lanes = lax.broadcasted_iota(jnp.int32, (SPILL, LANES), 1)
    zeros = jnp.zeros((SPILL, LANES), F32)

    def entry(k, q):
        return places[4 * k + q : 4 * k + q + 1, :]

    def scalar(k, q):
        return jnp.max(entry(k, q))

    def row_fade(k, first):
        i = lines + (first - entry(k, 0))
        return fade(i, (i >= entry(k, 2)) & (i < entry(k, 3)), tile)

    def col_fade(k, first):
        j = lanes[0:1] + (first - entry(k, 1))
        return fade(j, (j >= 0) & (j < tile), tile)

    def corrected(x, k, p):
        return terms[k, p : p + 1, :] * x + terms[k, 2 + p : 3 + p, :]

    left_rows, left_cols = scalar(1, 0), scalar(1, 1)
    up_rows, up_cols = scalar(2, 0), scalar(2, 1)
    corner_rows, corner_cols = scalar(3, 0), scalar(3, 1)
    moved_left[:, 0:SPILL, :] = jnp.zeros((PLANES, SPILL, LANES), F32)
    columns = [col_fade(0, v * LANES) for v in range(blocks)]
    left_column = col_fade(1, tile)

    def outgoing(first):
        here = pl.ds(first, rows)
        k = first // rows
        return (
            pltpu.make_async_copy(out.at[:, here, :], blended.at[:, here, :], sem.at[0, k]),
            pltpu.make_async_copy(out_weight.at[here, :], weights.at[here, :], sem.at[1, k]),
        )

    def turn_left(first):
        for p in range(PLANES):
            x = pltpu.roll(raw_left[p, pl.ds(first, rows), :].astype(F32), left_cols, 1)
            moved_left[p, pl.ds(first + SPILL, rows), :] = x

    def own_and_left(first):
        here = pl.ds(first, rows)
        own = row_fade(0, first)
        for v in range(blocks):
            weight = own * columns[v]
            part = slice(v * LANES, (v + 1) * LANES)
            values = [
                corrected(shifted[p, here, part].astype(F32), 0, p) * weight for p in range(PLANES)
            ]
            if v == 0:
                other = row_fade(1, first) * left_column
                weight = weight + other
                for p in range(PLANES):
                    x = moved_left[p, pl.ds(first + SPILL - left_rows, rows), :]
                    values[p] = values[p] + corrected(x, 1, p) * other
            out_weight[here, part] = weight
            for p in range(PLANES):
                out[p, here, part] = values[p]

    for k in range(SPILL // rows):
        turn_left(k * rows)

    def below(k, carry):
        first = pl.multiple_of(k * rows, rows)
        turn_left(first)
        own_and_left(first)
        for copy in outgoing(first):
            copy.start()
        return carry

    lax.fori_loop(SPILL // rows, count, below, 0)

    for p in range(PLANES):
        before = None
        for v in range(blocks):
            now = pltpu.roll(raw_up[p, :, v * LANES : (v + 1) * LANES].astype(F32), up_cols, 1)
            moved_up[p, v, 0:SPILL, :] = now if before is None else jnp.where(top_lanes < up_cols, before, now)
            moved_up[p, v, SPILL:, :] = zeros
            before = now
        moved_corner[p, 0:SPILL, :] = pltpu.roll(raw_corner[p].astype(F32), corner_cols, 1)
        moved_corner[p, SPILL:, :] = zeros
    up_columns = [col_fade(2, v * LANES) for v in range(blocks)]
    corner_column = col_fade(3, tile)
    for k in range(SPILL // rows):
        first = k * rows
        here = slice(first, first + rows)
        own_and_left(first)
        upper = row_fade(2, tile + first)
        for v in range(blocks):
            part = slice(v * LANES, (v + 1) * LANES)
            weight = upper * up_columns[v]
            out_weight[here, part] += weight
            for p in range(PLANES):
                x = moved_up[p, v, pl.ds(SPILL + first - up_rows, rows), :]
                out[p, here, part] += corrected(x, 2, p) * weight
        part = slice(0, LANES)
        weight = row_fade(3, tile + first) * corner_column
        out_weight[here, part] += weight
        for p in range(PLANES):
            x = moved_corner[p, pl.ds(SPILL + first - corner_rows, rows), :]
            out[p, here, part] += corrected(x, 3, p) * weight
        for copy in outgoing(first):
            copy.start()
    for k in range(count):
        for copy in outgoing(k * rows):
            copy.wait()


def blend(shifted, left_in, up_in, corner_in, terms, places):
    planes, tile, _ = shifted.shape
    blocks = tile // LANES
    return pl.pallas_call(
        blend_kernel,
        name="blend",
        out_shape=(
            jax.ShapeDtypeStruct((planes, tile, tile), F32),
            jax.ShapeDtypeStruct((tile, tile), F32),
        ),
        in_specs=[pl.BlockSpec(memory_space=pltpu.VMEM)] * 6,
        out_specs=(pl.BlockSpec(memory_space=pl.ANY),) * 2,
        scratch_shapes=[
            pltpu.VMEM((planes, tile, tile), F32),
            pltpu.VMEM((tile, tile), F32),
            pltpu.VMEM((planes, SPILL + tile, LANES), F32),
            pltpu.VMEM((planes, blocks, 2 * SPILL, LANES), F32),
            pltpu.VMEM((planes, 2 * SPILL, LANES), F32),
            pltpu.SemaphoreType.DMA((2, tile // ROWS)),
        ],
        compiler_params=pltpu.CompilerParams(vmem_limit_bytes=32 * 1024 * 1024),
    )(shifted, left_in, up_in, corner_in, terms, places)


def local(tiles, extents, offsets, bands):
    return blend(*exchange(tiles, jnp.concatenate([extents, offsets, bands])))


def solution(mesh):
    return jax.shard_map(
        local,
        mesh=mesh,
        in_specs=(P(None, "row", "col"), P(), P(), P()),
        out_specs=(P(None, "row", "col"), P("row", "col")),
        check_vma=False,
    )
```

time: 39 us -> 28.5 us (0.73)
  the two profiles are of different devices: /device:TPU:26 before, /device:TPU:1 now
where the time goes in v3:
time: 28.5 us; the launch traced here: 28.3 us
  Pallas kernels  26.9 us (94%)
  other arithmetic  0.74 us (3%)
  between operations  0.64 us (2%)
    pallas_call x1, Pallas kernels, exchange(): pl.pallas_call(exchange_kernel, name='exchange', out_shape=(jax.ShapeDtyp...  21.6 us
    pallas_call x1, Pallas kernels, blend(): pl.pallas_call(blend_kernel, name='blend', out_shape=(jax.ShapeDtypeStruc...  5.31 us
    concatenate x1, other arithmetic, local(): return blend(*exchange(tiles, jnp.concatenate([extents, offsets, bands])))  0.74 us

profile of v3, /device:TPU:1, one launch (start us, length us, event | category | flops | bytes accessed | tf_op | source)
XLA Modules:
  0.0 28.3 jit_solution(4235208235419966042)
XLA Ops:
  0.6 0.7 %pad_add_fusion.settings_in = s32[6,8,16]{2,1,0:T(8,128)S(1)} fusion(s32[2,8,16]{2,1,0:T(8,128)} %param.7, s32[2,8,16]{2,1,0:T(8,128)} %param.6, s32[2,8,16]{2,1,0:T(8,128)} %param.5), kind=kLoop, calls=%fused_computation | loop fusion | flops 1536 | bytes 6144 | tf_op jit(solution)/shard_map/concatenate | solution.py:559
  1.4 21.6 %exchange.1 = (bf16[2,1024,1024]{2,1,0:T(8,128)(2,1)S(1)}, bf16[2,1024,128]{2,1,0:T(8,128)(2,1)S(1)}, bf16[2,128,1024]{2,1,0:T(8,128)(2,1)S(1)}, bf16[2,128,128]...) custom-call(s32[6,8,16]{2,1,0:T(8,128)S(1)} %pad_add_fusion.settings_in, ...), custom_call_target="tpu_custom_call" | custom-call | tf_op jit(solution)/shard_map/exchange/pallas_call | solution.py:374
  23.0 5.3 %blend.1 = (f32[2,1024,1024]{2,1,0:T(8,128)}, f32[1024,1024]{1,0:T(8,128)}) custom-call(bf16[2,1024,1024]{2,1,0:T(8,128)(2,1)S(1)} %get-tuple-element.8.shifted, bf16[2,1024,128]{2,1,0:T(8,128)(2,1)S(1)} %get-tuple-element.9.raw_left, bf16[2,128,1024]{2,1,0:T(8,128)(2,1)S(1)} %get-tuple-element.10.raw_up, ...), custom_call_target="tpu_custom_call" | custom-call | tf_op jit(solution)/shard_map/blend/pallas_call | solution.py:537

commit v4 on v3

--- a/solution.py
+++ b/solution.py
@@ -11,6 +11,7 @@
 LANES = 128
 ROWS = 64
 PLANES = 2
+TILE = 1024
 EPS = 1e-6
 MESH = pl.DeviceIdType.MESH
 F32 = jnp.float32
@@ -23,6 +24,7 @@
     for c in range(-3, 3)
     if min(abs(r - a) + abs(c - b) for a, b in BLENDED) <= 2 and (r, c) != (0, 0)
 )
+SOURCES = tuple(sorted(SOURCES, key=lambda d: (-abs(d[0]) - abs(d[1]), d)))
 RIGHT_1, LEFT_1, DOWN_1, UP_1, RIGHT_2, DOWN_2, CORNER = range(7)
 
 
@@ -112,10 +114,25 @@
     return tuple((across[k] + along[k] - back[k] - above[k]) / scale for k in (1, 2))
 
 
+def fade(ids, limit, tile):
+    steps = jnp.minimum(ids, tile - 1 - ids) + 1
+    return jnp.where(limit, steps.astype(F32) * (2.0 / tile), 0.0)
+
+
+def row_fade(places, k, lines):
+    i = lines - places[4 * k : 4 * k + 1, :]
+    return fade(i, (i >= places[4 * k + 2 : 4 * k + 3, :]) & (i < places[4 * k + 3 : 4 * k + 4, :]), TILE)
+
+
+def col_fade(places, k, columns):
+    j = columns - places[4 * k + 1 : 4 * k + 2, :]
+    return fade(j, (j >= 0) & (j < TILE), TILE)
+
+
 def exchange_kernel(
-    settings_in, tiles, shifted, left_in, up_in, corner_in, terms, places,
+    settings_in, tiles, shifted, total_weight, left_in, up_in, corner_in, terms, places,
     settings, raw, half_r, half_d, moved, stats_out, stats_in, sums_out, sums_in,
-    load_sem, send_sem, recv_sem, mean_send, mean_recv, sums_send, sums_recv,
+    load_sem, send_sem, recv_sem, mean_send, mean_recv, sums_send, sums_recv, rounds,
 ):
     n_col, n_row = lax.axis_size("col"), lax.axis_size("row")
     col, row = lax.axis_index("col"), lax.axis_index("row")
@@ -134,15 +151,16 @@
     sums_in[...] = jnp.zeros_like(sums_in)
     stats_in[...] = jnp.zeros_like(stats_in)
 
+    def tell(semaphore):
+        for r, c in four:
+
+            @pl.when(exists(r, c))
+            def _(r=r, c=c):
+                pl.semaphore_signal(semaphore, inc=1, device_id=place(r, c), device_id_type=MESH)
+
+    neighbours = sum(exists(r, c).astype(jnp.int32) for r, c in four)
     barrier = pltpu.get_barrier_semaphore()
-    expected = 0
-    for r, c in SOURCES:
-
-        @pl.when(exists(r, c))
-        def _(r=r, c=c):
-            pl.semaphore_signal(barrier, inc=1, device_id=place(r, c), device_id_type=MESH)
-
-        expected = expected + exists(-r, -c).astype(jnp.int32)
+    tell(barrier)
 
     fetch = pltpu.make_async_copy(settings_in, settings, load_sem.at[blocks])
     fetch.start()
@@ -152,7 +170,7 @@
         loads.append(pltpu.make_async_copy(tiles.at[:, part, :], raw.at[:, part, :], load_sem.at[k]))
         loads[k].start()
 
-    pl.semaphore_wait(barrier, expected)
+    pl.semaphore_wait(barrier, neighbours)
 
     class Remote:
         def __init__(self, src, dst, send, recv, r, c, wanted=True):
@@ -199,6 +217,7 @@
     numbers = [(e * tile).astype(F32) for e in ext]
     one = lax.broadcasted_iota(jnp.int32, (1, LANES), 1)
 
+    tell(rounds.at[0])
     for load in loads:
         load.wait()
 
@@ -221,6 +240,9 @@
             count_row = jnp.where(one == 64 * p + 3 * side + 2, numbers[side], count_row)
             own_means.append(mean)
         means.append(own_means)
+        if side in (1, 3):
+            pl.semaphore_wait(rounds.at[side // 2], neighbours)
+            tell(rounds.at[side // 2 + 1])
     stats_out[...] = packed
     opposite = (1, 0, 3, 2)
     early = []
@@ -235,6 +257,36 @@
 
     dy, dx = settings[2, row, col], settings[3, row, col]
     wide = lax.broadcasted_iota(jnp.int32, (BLOCK, LANES), 1)
+
+    def weigh():
+        size = 64
+        lines = lax.broadcasted_iota(jnp.int32, (size, LANES), 0)
+        columns = lax.broadcasted_iota(jnp.int32, (1, LANES), 1)
+        own = [col_fade(places, 0, columns + v * LANES) for v in range(blocks)]
+        side = col_fade(places, 1, columns + tile)
+
+        def body(k, carry):
+            here = pl.ds(pl.multiple_of(k * size, size), size)
+            fades = row_fade(places, 0, lines + k * size)
+            beside = row_fade(places, 1, lines + k * size)
+            for v in range(blocks):
+                weight = fades * own[v]
+                if v == 0:
+                    weight = weight + beside * side
+                total_weight[here, v * LANES : (v + 1) * LANES] = weight
+            return carry
+
+        lax.fori_loop(0, tile // size, body, 0)
+        above = [col_fade(places, 2, columns + v * LANES) for v in range(blocks)]
+        corner = col_fade(places, 3, columns + tile)
+        for first in range(0, SPILL, size):
+            fades = row_fade(places, 2, lines + (tile + first))
+            beside = row_fade(places, 3, lines + (tile + first))
+            for v in range(blocks):
+                weight = fades * above[v]
+                if v == 0:
+                    weight = weight + beside * corner
+                total_weight[first : first + size, v * LANES : (v + 1) * LANES] += weight
 
     def shift_plane(p):
         moved[:, 0:SPILL, :] = jnp.zeros((blocks, SPILL, LANES), F32)
@@ -280,7 +332,9 @@
             ref[...] = jnp.zeros_like(ref)
 
     shift_plane(0)
-
+    weigh()
+
+    pl.semaphore_wait(rounds.at[2], neighbours)
     for copy in early:
         copy.wait_recv()
 
@@ -376,6 +430,7 @@
         name="exchange",
         out_shape=(
             jax.ShapeDtypeStruct((planes, tile, tile), dtype),
+            jax.ShapeDtypeStruct((tile, tile), F32),
             jax.ShapeDtypeStruct((planes, tile, STRIP), dtype),
             jax.ShapeDtypeStruct((planes, STRIP, tile), dtype),
             jax.ShapeDtypeStruct((planes, STRIP, STRIP), dtype),
@@ -383,7 +438,7 @@
             jax.ShapeDtypeStruct((16, LANES), jnp.int32),
         ),
         in_specs=[pl.BlockSpec(memory_space=pl.ANY)] * 2,
-        out_specs=(in_vmem,) * 6,
+        out_specs=(in_vmem,) * 7,
         scratch_shapes=[
             pltpu.SMEM(settings.shape, settings.dtype),
             pltpu.VMEM((planes, tile, tile), dtype),
@@ -401,22 +456,20 @@
             dma((4,)),
             dma((len(SOURCES),)),
             dma((len(SOURCES),)),
+            pltpu.SemaphoreType.REGULAR((3,)),
         ],
         compiler_params=pltpu.CompilerParams(
-            collective_id=0, has_side_effects=True, vmem_limit_bytes=48 * 1024 * 1024
+            collective_id=0, has_side_effects=True, vmem_limit_bytes=44 * 1024 * 1024
         ),
     )(settings, tiles)
 
 
-def fade(ids, limit, tile):
-    steps = jnp.minimum(ids, tile - 1 - ids) + 1
-    return jnp.where(limit, steps.astype(F32) * (2.0 / tile), 0.0)
-
-
 def blend_kernel(
-    shifted, raw_left, raw_up, raw_corner, terms, places, blended, weights,
-    out, out_weight, moved_left, moved_up, moved_corner, sem,
+    shifted, total_weight, raw_left, raw_up, raw_corner, terms, places, blended, weights,
+    out, moved_left, moved_up, moved_corner, sem,
 ):
+    whole = pltpu.make_async_copy(total_weight, weights, sem.at[weights.shape[0] // ROWS])
+    whole.start()
     tile = weights.shape[0]
     rows = ROWS
     count = tile // rows
@@ -426,19 +479,8 @@
     top_lanes = lax.broadcasted_iota(jnp.int32, (SPILL, LANES), 1)
     zeros = jnp.zeros((SPILL, LANES), F32)
 
-    def entry(k, q):
-        return places[4 * k + q : 4 * k + q + 1, :]
-
     def scalar(k, q):
-        return jnp.max(entry(k, q))
-
-    def row_fade(k, first):
-        i = lines + (first - entry(k, 0))
-        return fade(i, (i >= entry(k, 2)) & (i < entry(k, 3)), tile)
-
-    def col_fade(k, first):
-        j = lanes[0:1] + (first - entry(k, 1))
-        return fade(j, (j >= 0) & (j < tile), tile)
+        return jnp.max(places[4 * k + q : 4 * k + q + 1, :])
 
     def corrected(x, k, p):
         return terms[k, p : p + 1, :] * x + terms[k, 2 + p : 3 + p, :]
@@ -447,16 +489,12 @@
     up_rows, up_cols = scalar(2, 0), scalar(2, 1)
     corner_rows, corner_cols = scalar(3, 0), scalar(3, 1)
     moved_left[:, 0:SPILL, :] = jnp.zeros((PLANES, SPILL, LANES), F32)
-    columns = [col_fade(0, v * LANES) for v in range(blocks)]
-    left_column = col_fade(1, tile)
+    columns = [col_fade(places, 0, lanes[0:1] + v * LANES) for v in range(blocks)]
+    left_column = col_fade(places, 1, lanes[0:1] + tile)
 
     def outgoing(first):
         here = pl.ds(first, rows)
-        k = first // rows
-        return (
-            pltpu.make_async_copy(out.at[:, here, :], blended.at[:, here, :], sem.at[0, k]),
-            pltpu.make_async_copy(out_weight.at[here, :], weights.at[here, :], sem.at[1, k]),
-        )
+        return pltpu.make_async_copy(out.at[:, here, :], blended.at[:, here, :], sem.at[first // rows])
 
     def turn_left(first):
         for p in range(PLANES):
@@ -465,7 +503,7 @@
 
     def own_and_left(first):
         here = pl.ds(first, rows)
-        own = row_fade(0, first)
+        own = row_fade(places, 0, lines + first)
         for v in range(blocks):
             weight = own * columns[v]
             part = slice(v * LANES, (v + 1) * LANES)
@@ -473,12 +511,10 @@
                 corrected(shifted[p, here, part].astype(F32), 0, p) * weight for p in range(PLANES)
             ]
             if v == 0:
-                other = row_fade(1, first) * left_column
-                weight = weight + other
+                other = row_fade(places, 1, lines + first) * left_column
                 for p in range(PLANES):
                     x = moved_left[p, pl.ds(first + SPILL - left_rows, rows), :]
                     values[p] = values[p] + corrected(x, 1, p) * other
-            out_weight[here, part] = weight
             for p in range(PLANES):
                 out[p, here, part] = values[p]
 
@@ -489,8 +525,7 @@
         first = pl.multiple_of(k * rows, rows)
         turn_left(first)
         own_and_left(first)
-        for copy in outgoing(first):
-            copy.start()
+        outgoing(first).start()
         return carry
 
     lax.fori_loop(SPILL // rows, count, below, 0)
@@ -504,34 +539,31 @@
             before = now
         moved_corner[p, 0:SPILL, :] = pltpu.roll(raw_corner[p].astype(F32), corner_cols, 1)
         moved_corner[p, SPILL:, :] = zeros
-    up_columns = [col_fade(2, v * LANES) for v in range(blocks)]
-    corner_column = col_fade(3, tile)
+    up_columns = [col_fade(places, 2, lanes[0:1] + v * LANES) for v in range(blocks)]
+    corner_column = col_fade(places, 3, lanes[0:1] + tile)
     for k in range(SPILL // rows):
         first = k * rows
         here = slice(first, first + rows)
         own_and_left(first)
-        upper = row_fade(2, tile + first)
+        upper = row_fade(places, 2, lines + (tile + first))
         for v in range(blocks):
             part = slice(v * LANES, (v + 1) * LANES)
             weight = upper * up_columns[v]
-            out_weight[here, part] += weight
             for p in range(PLANES):
                 x = moved_up[p, v, pl.ds(SPILL + first - up_rows, rows), :]
                 out[p, here, part] += corrected(x, 2, p) * weight
         part = slice(0, LANES)
-        weight = row_fade(3, tile + first) * corner_column
-        out_weight[here, part] += weight
+        weight = row_fade(places, 3, lines + (tile + first)) * corner_column
         for p in range(PLANES):
             x = moved_corner[p, pl.ds(SPILL + first - corner_rows, rows), :]
             out[p, here, part] += corrected(x, 3, p) * weight
-        for copy in outgoing(first):
-            copy.start()
+        outgoing(first).start()
     for k in range(count):
-        for copy in outgoing(k * rows):
-            copy.wait()
-
-
-def blend(shifted, left_in, up_in, corner_in, terms, places):
+        outgoing(k * rows).wait()
+    whole.wait()
+
+
+def blend(shifted, total_weight, left_in, up_in, corner_in, terms, places):
     planes, tile, _ = shifted.shape
     blocks = tile // LANES
     return pl.pallas_call(
@@ -541,18 +573,17 @@
             jax.ShapeDtypeStruct((planes, tile, tile), F32),
             jax.ShapeDtypeStruct((tile, tile), F32),
         ),
-        in_specs=[pl.BlockSpec(memory_space=pltpu.VMEM)] * 6,
+        in_specs=[pl.BlockSpec(memory_space=pltpu.VMEM)] * 7,
         out_specs=(pl.BlockSpec(memory_space=pl.ANY),) * 2,
         scratch_shapes=[
             pltpu.VMEM((planes, tile, tile), F32),
-            pltpu.VMEM((tile, tile), F32),
             pltpu.VMEM((planes, SPILL + tile, LANES), F32),
             pltpu.VMEM((planes, blocks, 2 * SPILL, LANES), F32),
             pltpu.VMEM((planes, 2 * SPILL, LANES), F32),
-            pltpu.SemaphoreType.DMA((2, tile // ROWS)),
+            pltpu.SemaphoreType.DMA((tile // ROWS + 1,)),
         ],
         compiler_params=pltpu.CompilerParams(vmem_limit_bytes=32 * 1024 * 1024),
-    )(shifted, left_in, up_in, corner_in, terms, places)
+    )(shifted, total_weight, left_in, up_in, corner_in, terms, places)
 
 
 def local(tiles, extents, offsets, bands):

time: 28.5 us -> 26.3 us (0.923)
  Pallas kernels: 26.9 us -> 24.7 us
    pallas_call x1, Pallas kernels: 21.6 us -> 20 us  [exchange(): pl.pallas_call(exchange_kernel, name='exchange', out_shape=(jax.ShapeDtyp...]
    pallas_call x1, Pallas kernels: 5.31 us -> 4.71 us  [blend(): pl.pallas_call(blend_kernel, name='blend', out_shape=(jax.ShapeDtypeStruc...]
where the time goes in v4:
time: 26.3 us; the launch traced here: 26.1 us
  Pallas kernels  24.7 us (94%)
  other arithmetic  0.74 us (3%)
  between operations  0.64 us (2%)
    pallas_call x1, Pallas kernels, exchange(): pl.pallas_call(exchange_kernel, name='exchange', out_shape=(jax.ShapeDtyp...  20 us
    pallas_call x1, Pallas kernels, blend(): pl.pallas_call(blend_kernel, name='blend', out_shape=(jax.ShapeDtypeStruc...  4.71 us
    concatenate x1, other arithmetic, local(): return blend(*exchange(tiles, jnp.concatenate([extents, offsets, bands])))  0.74 us

profile of v4, /device:TPU:1, one launch (start us, length us, event | category | flops | bytes accessed | tf_op | source)
XLA Modules:
  0.0 26.1 jit_solution(5282777618372886223)
XLA Ops:
  0.6 0.7 %pad_add_fusion.settings_in = s32[6,8,16]{2,1,0:T(8,128)S(1)} fusion(s32[2,8,16]{2,1,0:T(8,128)} %param.7, s32[2,8,16]{2,1,0:T(8,128)} %param.6, s32[2,8,16]{2,1,0:T(8,128)} %param.5), kind=kLoop, calls=%fused_computation | loop fusion | flops 1536 | bytes 6144 | tf_op jit(solution)/shard_map/concatenate | solution.py:590
  1.4 20.0 %exchange.1 = (bf16[2,1024,1024]{2,1,0:T(8,128)(2,1)S(1)}, f32[1024,1024]{1,0:T(8,128)S(1)}, bf16[2,1024,128]{2,1,0:T(8,128)(2,1)S(1)}, bf16[2,128,1024]{2,1,0:T...) custom-call(s32[6,8,16]{2,1,0:T(8,128)S(1)} %pad_add_fusion.settings_in, ...), custom_call_target="tpu_custom_call" | custom-call | tf_op jit(solution)/shard_map/exchange/pallas_call | solution.py:428
  21.4 4.7 %blend.1 = (f32[2,1024,1024]{2,1,0:T(8,128)}, f32[1024,1024]{1,0:T(8,128)}) custom-call(bf16[2,1024,1024]{2,1,0:T(8,128)(2,1)S(1)} %get-tuple-element.9.shifted, f32[1024,1024]{1,0:T(8,128)S(1)} %get-tuple-element.10.total_weight, bf16[2,1024,128]{2,1,0:T(8,128)(2,1)S(1)} %get-tuple-element.11.raw_left, bf16[2,128,1024]{2,1,0:T(8,128)(2,1)S(1)} %get-tuple-element.12.raw_up, ...), custom_call_target="tpu_custom_call" | custom-call | tf_op jit(solution)/shard_map/blend/pallas_call | solution.py:569
